TPU v7x, 256 devices: a whole 4x4x8 slice. The times are simulated.
256 devices in a mesh: dp: 8 (over x, z_hi), ctx: 32 (over y, z_lo, core).
Axes of the slice: x: 4, y: 4, z: 8 (z_hi: 2, z_lo: 4; z = z_hi * 4 + z_lo), core: 2. Of those that a mesh axis runs over, the one named last changes fastest.
Arguments:
- layer_input: bfloat16 [8, 4096, 8192], P('dp', 'ctx'), may hold values from -6 to 6
- queries: bfloat16 [8, 4096, 1024], P('dp', 'ctx'), may hold values from -6 to 6
- keys: bfloat16 [8, 4096, 128], P('dp', 'ctx'), may hold values from -6 to 6
- values: bfloat16 [8, 4096, 128], P('dp', 'ctx'), may hold values from -6 to 6
- d_out: bfloat16 [8, 4096, 1024], P('dp', 'ctx'), may hold values from -6 to 6
- doc_lengths: int32 [8, 8], P('dp'), may hold values from 1 to 1024, 4096 in all within a row
- block_order: int32 [64], replicated, may hold values from 0 to 63, as said below
Outputs:
- query_grad: bfloat16 [8, 4096, 1024], P('dp', 'ctx')
- key_grad: bfloat16 [8, 4096, 128], P('dp', 'ctx')
- value_grad: bfloat16 [8, 4096, 128], P('dp', 'ctx')
- kv_weight_grad: float32 [32, 256, 256], P('ctx', 'dp')
Inputs may be any that keep to these rules, and one draw needn't show every extreme that they name: `block_order`: entries 2r and 2r+1 are the blocks stored in rows 2r*64 to 2r*64 + 2*64 - 1; they sum to 63, and every block appears once.
All inputs are finite; a program needn't handle non-finite values.
Results may differ from a plain program's by a relative error of at most 0.012.
Values may be sent and summed in bfloat16 or wider, within the bound.
A program may use at most 64 MiB of HBM per device.

v0:
```python
import math

import jax
import jax.numpy as jnp
from jax import lax
from jax.sharding import PartitionSpec as P

big_negative = -1e30


def per_device(layer_input, queries, keys, values, d_out, doc_lengths, block_order):
    local_len = queries.shape[1]
    head_dim = keys.shape[2]
    heads = queries.shape[2] // head_dim
    ctx_size = lax.axis_size("ctx")
    seq_len = local_len * ctx_size
    half = local_len // 2
    rank = lax.axis_index("ctx")
    scale = 1.0 / math.sqrt(head_dim)
    key_pos = (block_order[:, None] * half + jnp.arange(half, dtype=jnp.int32)[None, :]).reshape(
        seq_len
    )
    ends = jnp.cumsum(doc_lengths[0])
    key_doc = jnp.sum((key_pos[:, None] >= ends[None, :]).astype(jnp.int32), axis=1)
    query_pos = lax.dynamic_slice_in_dim(key_pos, rank * local_len, local_len)
    query_doc = lax.dynamic_slice_in_dim(key_doc, rank * local_len, local_len)
    local_rows = layer_input[0]
    all_keys, all_values = (
        lax.all_gather(keys[0], "ctx", axis=0, tiled=True),
        lax.all_gather(values[0], "ctx", axis=0, tiled=True),
    )
    block = 512
    nblocks = seq_len // block
    key_blocks = all_keys.reshape(nblocks, block, head_dim)
    value_blocks = all_values.reshape(nblocks, block, head_dim)
    pos_blocks = key_pos.reshape(nblocks, block)
    doc_blocks = key_doc.reshape(nblocks, block)
    q_heads = queries[0].reshape(local_len, heads, head_dim)
    d_heads = d_out[0].reshape(local_len, heads, head_dim)

    def visible(kpos, kdoc):
        return ((kpos[None, :] <= query_pos[:, None]) & (kdoc[None, :] == query_doc[:, None]))[None]

    def scores(kblock):
        return (
            jnp.einsum("thd,kd->htk", q_heads, kblock, preferred_element_type=jnp.float32) * scale
        )

    def prob_grads(vblock):
        return jnp.einsum("thd,kd->htk", d_heads, vblock, preferred_element_type=jnp.float32)

    def stats_step(carry, item):
        run_max, run_sum, run_dot = carry
        kblock, vblock, kpos, kdoc = item
        mask = visible(kpos, kdoc)
        s = scores(kblock)
        new_max = jnp.maximum(run_max, jnp.max(jnp.where(mask, s, big_negative), axis=2))
        terms = jnp.where(mask, jnp.exp(s - new_max[..., None]), 0.0)
        factor = jnp.exp(run_max - new_max)
        run_sum = run_sum * factor + jnp.sum(terms, axis=2)
        run_dot = run_dot * factor + jnp.sum(terms * prob_grads(vblock), axis=2)
        return ((new_max, run_sum, run_dot), None)

    items = (key_blocks, value_blocks, pos_blocks, doc_blocks)
    zeros_stat = jnp.zeros((heads, local_len), jnp.float32)
    start_stats = (jnp.full((heads, local_len), big_negative, jnp.float32), zeros_stat, zeros_stat)
    (run_max, run_sum, run_dot), _ = lax.scan(stats_step, start_stats, items)
    lse = run_max + jnp.log(run_sum)
    delta = run_dot / run_sum

    def grad_step(dq_acc, item):
        kblock, vblock, kpos, kdoc = item
        p = jnp.where(visible(kpos, kdoc), jnp.exp(scores(kblock) - lse[..., None]), 0.0)
        weights = p.astype(jnp.bfloat16)
        dprob = prob_grads(vblock)
        dscore = (p * (dprob - delta[..., None])).astype(jnp.bfloat16)
        dq_acc = dq_acc + jnp.einsum(
            "htk,kd->thd", dscore, kblock, preferred_element_type=jnp.float32
        )
        dk_part = (
            jnp.einsum("htk,thd->kd", dscore, q_heads, preferred_element_type=jnp.float32) * scale
        )
        dv_part = jnp.einsum("htk,thd->kd", weights, d_heads, preferred_element_type=jnp.float32)
        return (dq_acc, jnp.concatenate([dk_part, dv_part], axis=1))

    dq_acc, partials = lax.scan(
        grad_step, jnp.zeros((local_len, heads, head_dim), jnp.float32), items
    )
    owned = lax.psum_scatter(
        partials.reshape(seq_len, 2 * head_dim), "ctx", scatter_dimension=0, tiled=True
    )
    kv_grad = owned.astype(jnp.bfloat16)
    query_grad = (dq_acc * scale).astype(jnp.bfloat16).reshape(1, local_len, heads * head_dim)
    contract = (((0,), (0,)), ((), ()))
    exact = lax.Precision.HIGHEST
    cols = local_rows.astype(jnp.float32)
    term = lax.psum_scatter(
        lax.dot_general(cols, owned, contract, precision=exact, preferred_element_type=jnp.float32),
        "ctx",
        scatter_dimension=0,
        tiled=True,
    )
    weight_grad = lax.psum_scatter(term, "dp", scatter_dimension=0, tiled=True)
    weight_grad = weight_grad * (1.0 / math.sqrt(lax.axis_size("dp") * seq_len))
    key_grad = kv_grad[:, :head_dim].reshape(1, local_len, head_dim)
    value_grad = kv_grad[:, head_dim:].reshape(1, local_len, head_dim)
    return (
        query_grad,
        key_grad,
        value_grad,
        weight_grad.reshape(1, weight_grad.shape[0], 2 * head_dim),
    )


def solution(mesh):
    placed = (
        P("dp", "ctx", None),
        P("dp", "ctx", None),
        P("dp", "ctx", None),
        P("dp", "ctx", None),
        P("dp", "ctx", None),
        P("dp", None),
        P(),
    )
    return jax.shard_map(
        per_device,
        mesh=mesh,
        in_specs=placed,
        out_specs=(
            P("dp", "ctx", None),
            P("dp", "ctx", None),
            P("dp", "ctx", None),
            P("ctx", "dp", None),
        ),
        check_vma=False,
    )
```

profile of v0, /device:TPU:1, one launch (start us, length us, event | category | flops | bytes accessed | tf_op | source)
XLA Modules:
  0.0 635.3 jit_solution(2492663735038133514)
XLA Ops:
  11.0 1.8 copy.43
  15.2 57.8 %all-gather.5.cloned.1.call-done = bf16[1,4096,128]{2,1,0:T(8,128)(2,1)} async-done(((bf16[1,128,128]{2,1,0:T(8,128)(2,1)}), bf16[1,4096,128]{2,1,0:T(8,128)(2,1)}) %all-gather.5.cloned.1.call-update) | async-done | bytes 1048592 | tf_op jit(solution)/shard_map/all_gather | solution.py:29
  73.0 59.7 %all-gather.7.cloned.1.call-done = bf16[1,4096,128]{2,1,0:T(8,128)(2,1)} async-done(((bf16[1,128,128]{2,1,0:T(8,128)(2,1)}), bf16[1,4096,128]{2,1,0:T(8,128)(2,1)}) %all-gather.7.cloned.1.call-update) | async-done | bytes 1048592 | tf_op jit(solution)/shard_map/all_gather | solution.py:30
  132.7 29.4 %while.28 = (s32[]{:T(128)}, f32[8,128]{1,0:T(8,128)S(1)}, f32[8,128]{1,0:T(8,128)S(1)}, f32[8,128]{1,0:T(8,128)S(1)}, s32[8,512]{1,0:T(8,128)S(1)}, /*index=5*/...) while((s32[]{:T(128)}, f32[8,128]{1,0:T(8,128)S(1)}, ...), condition=%wide.region_6.7_spmd.clone, body=%wide.region_2.6_spmd.clone.sunk | while | flops 274930688 | bytes 7427236 | solution.py:67
  134.3 1.6 fusion.66
  138.0 1.6 fusion.66
  141.7 1.6 fusion.66
  145.3 1.6 fusion.66
  149.0 1.6 fusion.66
  152.7 1.6 fusion.66
  162.1 67.4 %while.29 = (s32[]{:T(128)}, f32[128,8,128]{0,2,1:T(8,128)}, f32[8,512,256]{2,1,0:T(8,128)}, bf16[8,512,128]{2,1,0:T(8,128)(2,1)}, s32[8,512]{1,0:T(8,128)S(1)},...) while((s32[]{:T(128)}, f32[128,8,128]{0,2,1:T(8,128)}, ...), condition=%wide.region_8.9_spmd.clone, body=%wide.region_7.8_spmd.clone.sunk | while | flops 675414016 | bytes 15750323 | solution.py:86
  162.3 1.6 fusion.79
  167.2 2.1 fusion.81
  170.5 1.6 fusion.79
  175.4 2.3 fusion.81
  179.0 1.6 fusion.79
  183.8 2.3 fusion.81
  187.4 1.6 fusion.79
  192.3 2.3 fusion.81
  195.9 1.6 fusion.79
  200.7 2.3 fusion.81
  204.3 1.6 fusion.79
  209.2 2.3 fusion.81
  212.8 1.6 fusion.79
  217.6 2.3 fusion.81
  221.2 1.6 fusion.79
  226.0 2.3 fusion.81
  229.5 146.7 %reduce-scatter.6.cloned.1.call-done = f32[128,256]{1,0:T(8,128)} async-done(((f32[4096,256]{1,0:T(8,128)}), f32[128,256]{1,0:T(8,128)}) %reduce-scatter.6.cloned.1.call-update) | async-done | bytes 131088 | tf_op jit(solution)/shard_map/reduce_scatter | solution.py:89
  376.2 6.6 %convolution_bitcast_fusion.3 = f32[8192,256]{0,1:T(8,128)} fusion(f32[128,256]{1,0:T(8,128)} %reduce-scatter.6.cloned.1.call-done, bf16[1,128,8192]{2,1,0:T(8,128)(2,1)S(1)} %copy-done), kind=kOutput, calls=%fused_computation.50 | convolution fusion | flops 3221225472 | bytes 10616832 | tf_op jit(solution)/shard_map/dot_general | solution.py:98
  382.9 159.7 %reduce-scatter.8.cloned.1.call-done = f32[256,256]{0,1:T(8,128)} async-done(((f32[8192,256]{0,1:T(8,128)}), f32[256,256]{0,1:T(8,128)}) %reduce-scatter.8.cloned.1.call-update) | async-done | bytes 262160 | tf_op jit(solution)/shard_map/reduce_scatter | solution.py:97
  542.6 1.8 copy.58
  547.0 80.2 %reduce-scatter.10.cloned.1.call-done = f32[32,256]{1,0:T(8,128)} async-done(((f32[256,256]{1,0:T(8,128)}), f32[32,256]{1,0:T(8,128)}) %reduce-scatter.10.cloned.1.call-update) | async-done | bytes 32784
  (166 shorter events, 65.9 us)
Async XLA Ops:
  7.2 369.1 %copy-start = (bf16[1,128,8192]{2,1,0:T(8,128)(2,1)S(1)}, bf16[1,128,8192]{2,1,0:T(8,128)(2,1)}, u32[]{:S(2)}) copy-start(bf16[1,128,8192]{2,1,0:T(8,128)(2,1)} %param.11) | copy-start | bytes 6291460
  7.2 65.9 %all-gather.5.cloned.1.call-start = ((), (), s32[]{:S(2)}) async-start(), calls=%async_computation.5 | async-start | bytes 1081344 | tf_op jit(solution)/shard_map/all_gather | solution.py:29
  7.9 124.8 %all-gather.7.cloned.1.call-start = ((), (), s32[]{:S(2)}) async-start(), calls=%async_computation.6 | async-start | bytes 1081344 | tf_op jit(solution)/shard_map/all_gather | solution.py:30
  8.7 367.6 %reduce-scatter.6.cloned.1.call-start = ((), (), s32[]{:S(2)}) async-start(), calls=%async_computation.3 | async-start | bytes 4325376 | tf_op jit(solution)/shard_map/reduce_scatter | solution.py:89
  229.5 313.2 %reduce-scatter.8.cloned.1.call-start = ((), (), s32[]{:S(2)}) async-start(), calls=%async_computation.4 | async-start | bytes 8650752 | tf_op jit(solution)/shard_map/reduce_scatter | solution.py:97
  382.8 163.5 %copy-start.1 = (f32[128,256]{1,0:T(8,128)S(1)}, f32[128,256]{1,0:T(8,128)}, u32[]{:S(2)}) copy-start(f32[128,256]{1,0:T(8,128)} %reduce-scatter.6.cloned.1.call-done) | copy-start | bytes 393220
  382.8 244.4 %reduce-scatter.10.cloned.1.call-start = ((), (), s32[]{:S(2)}) async-start(), calls=%async_computation.7 | async-start | bytes 294912
Sparse Core Ops, SparseCore 0:
  9.9 63.1 all-gather.4
  74.9 57.7 all-gather.6
  229.6 146.5 reduce-scatter.5
  382.9 159.6 reduce-scatter.7
  546.3 80.8 reduce-scatter.9
where the time goes:
time: 638 us; the launch traced here: 635 us
  waiting for transfers between devices  506 us (79%)
  matrix products  86.7 us (14%)
  local copies, waits for them, and re-layouts  18 us (3%)
  between operations  13.9 us (2%)
  other arithmetic  9.99 us (2%)
    reduce_scatter x1, waiting for transfers between devices, per_device(): lax.psum_scatter(lax.dot_general(cols, owned, contract, precision=exact,...  160 us
    reduce_scatter x1, waiting for transfers between devices, per_device(): lax.psum_scatter(partials.reshape(seq_len, 2 * head_dim), 'ctx', scatter_...  147 us
    unnamed x6, waiting for transfers between devices  81.6 us
    all_gather x1, waiting for transfers between devices, per_device(): lax.all_gather(values[0], 'ctx', axis=0, tiled=True)  59.7 us
    all_gather x1, waiting for transfers between devices, per_device(): lax.all_gather(keys[0], 'ctx', axis=0, tiled=True)  57.8 us
    dot_general x16, matrix products, scores(): jnp.einsum('thd,kd->htk', q_heads, kblock, preferred_element_type=jnp.flo...  23.5 us
    dot_general x16, matrix products, prob_grads(): jnp.einsum('thd,kd->htk', d_heads, vblock, preferred_element_type=jnp.flo...  23.1 us
    dot_general x8, matrix products, grad_step(): jnp.einsum('htk,kd->thd', dscore, kblock, preferred_element_type=jnp.floa...  18.3 us
  transfers between devices with their start and end apart: 5, of which 5 were waited for; matrix products, arithmetic and copies ran while one was open for 1% of the time, Pallas kernels for 0%

commit v1 on v0

v1 whole, which is shorter than its diff:
```python
import math

import jax
import jax.numpy as jnp
from jax import lax
from jax.experimental import pallas as pl
from jax.experimental.pallas import tpu as pltpu
from jax.sharding import PartitionSpec as P

NX, NY, NZL, NZH, NC = 4, 4, 4, 2, 2
NCTX = NY * NZL * NC
ROWS = 128
HD = 128
HEADS = 8
HALF = 64
BLOCKS = 64
SEQ = 4096
D = 8192
NDOCS = 8
XC = NX * NC
DCOLS = D // XC
CHUNK = 256
PER_CHUNK = CHUNK // HALF
MAX_CHUNKS = 5
QCOLS = HEADS * HALF
SCALE = 1.0 / math.sqrt(HD)
LOG2E = math.log2(math.e)
HIDDEN = -1e30
MESH = pl.DeviceIdType.MESH
F32 = jnp.float32
BF16 = jnp.bfloat16
NT = (((1,), (1,)), ((), ()))
TN = (((0,), (0,)), ((), ()))


def place():
    dp = lax.axis_index("dp")
    ctx = lax.axis_index("ctx")
    return dp // NZH, dp % NZH, ctx // (NZL * NC), (ctx // NC) % NZL, ctx % NC


def device(x, zh, y, zl, c):
    return (x * NZH + zh, (y * NZL + zl) * NC + c)


def remote(src, dst, send, recv, to):
    return pltpu.make_async_remote_copy(
        src_ref=src, dst_ref=dst, send_sem=send, recv_sem=recv, device_id=to, device_id_type=MESH
    )


def greet(peers):
    barrier = pltpu.get_barrier_semaphore()
    for peer in peers:
        pl.semaphore_signal(barrier, inc=1, device_id=peer, device_id_type=MESH)
    pl.semaphore_wait(barrier, len(peers))


def gather_kernel(k_ref, v_ref, x_hbm, kv_ref, xt_ref, xv, x_sem, zs, zr, ys, yr, cs, cr):
    x, zh, y, zl, c = place()

    def rank(q, p, core):
        return (((y - q + NY) % NY) * NZL + (zl - p + NZL) % NZL) * NC + core

    load_x = pltpu.make_async_copy(x_hbm.at[0], xv, x_sem)
    load_x.start()
    me = rank(0, 0, c)
    kv_ref[me, 0] = k_ref[0]
    kv_ref[me, 1] = v_ref[0]
    sibling = device(x, zh, y, zl, 1 - c)
    y_peers = [device(x, zh, (y + o) % NY, zl, c) for o in range(1, NY)]
    z_peers = [device(x, zh, y, (zl + o) % NZL, c) for o in range(1, NZL)]
    greet([sibling] + y_peers + z_peers)
    sends = []

    def go(r, send, recv, to):
        copy = remote(kv_ref.at[r], kv_ref.at[r], send, recv, to)
        copy.start()
        sends.append(copy)

    def arrived(r, send, recv, to):
        remote(kv_ref.at[r], kv_ref.at[r], send, recv, to).wait_recv()

    for o in (2, 1, 3):
        go(me, zs.at[o - 1], zr.at[o - 1], z_peers[o - 1])
    for o in (2, 1, 3):
        go(me, ys.at[0, o - 1], yr.at[0, o - 1], y_peers[o - 1])
    go(me, cs.at[0, 0], cr.at[0, 0], sibling)

    load_x.wait()
    to_row = lax.broadcasted_iota(jnp.int32, (256, 256), 0)
    from_row = lax.broadcasted_iota(jnp.int32, (256, 256), 1)
    group = to_row // 64
    source = (group % 2) * 128 + (group // 2) * 64 + to_row % 64
    pick = jnp.where(source == from_row, 1.0, 0.0).astype(BF16)
    for k in range(NY * NZL // 2):
        for core in range(NC):
            for xh in range(NX // 2):
                at = 2 * k * 512 + core * 256 + xh * 128
                pair = jnp.concatenate([xv[:, at : at + 128], xv[:, at + 512 : at + 640]], axis=1)
                turned = lax.dot_general(pick, pair, NT, preferred_element_type=F32).astype(BF16)
                xt_ref[(2 * xh) * NC + core, k * 128 : (k + 1) * 128, :] = turned[:128]
                xt_ref[(2 * xh + 1) * NC + core, k * 128 : (k + 1) * 128, :] = turned[128:]

    for p in (1, 3, 2):
        r = rank(0, p, c)
        arrived(r, zs.at[p - 1], zr.at[p - 1], z_peers[p - 1])
        for o in (2, 1, 3):
            go(r, ys.at[p, o - 1], yr.at[p, o - 1], y_peers[o - 1])
        go(r, cs.at[0, p], cr.at[0, p], sibling)
    for p in (0, 1, 3, 2):
        for q in (1, 3, 2):
            r = rank(q, p, c)
            arrived(r, ys.at[p, q - 1], yr.at[p, q - 1], y_peers[q - 1])
            go(r, cs.at[q, p], cr.at[q, p], sibling)
    for p in range(NZL):
        for q in range(NY):
            arrived(rank(q, p, 1 - c), cs.at[q, p], cr.at[q, p], sibling)
    for copy in sends:
        copy.wait_send()


def attend_kernel(doc_ref, order_ref, q_ref, d_ref, kv_ref, dq_ref, part_ref, stored, acc, s_buf, g_buf, q8, d8, dq_acc):
    _, _, y, zl, c = place()
    r = (y * NZL + zl) * NC + c

    def invert(j, carry):
        stored[order_ref[j]] = j
        return carry

    lax.fori_loop(0, BLOCKS, invert, 0)

    def clear(j, carry):
        acc[j] = jnp.zeros((2, HALF, HD), F32)
        return carry

    lax.fori_loop(0, BLOCKS, clear, 0)
    ends = []
    end = 0
    for i in range(NDOCS):
        end = end + doc_ref[0, i]
        ends.append(end)

    for half in range(2):
        block = order_ref[2 * r + half]
        first = 0
        for end in ends:
            first = jnp.where(end <= block * HALF, end, first)
        block0 = first // HALF
        chunks = (block - block0) // PER_CHUNK + 1
        for h in range(HEADS):
            q8[h * HALF : (h + 1) * HALF, :] = q_ref[0, half * HALF : (half + 1) * HALF, h * HD : (h + 1) * HD]
            d8[h * HALF : (h + 1) * HALF, :] = d_ref[0, half * HALF : (half + 1) * HALF, h * HD : (h + 1) * HD]
        lane = lax.broadcasted_iota(jnp.int32, (1, 128), 1)
        query_pos = block * HALF + lane % HALF
        query_start = jnp.zeros((1, 128), jnp.int32)
        for end in ends:
            query_start = jnp.where(end <= query_pos, end, query_start)

        def places(ch):
            return [stored[jnp.minimum(block0 + ch * PER_CHUNK + t, BLOCKS - 1)] for t in range(PER_CHUNK)]

        def chunk_of(js, which):
            return jnp.concatenate([kv_ref[j // 2, which, j % 2] for j in js], axis=0)

        def score(ch, top):
            js = places(ch)
            s = lax.dot_general(chunk_of(js, 0), q8[...], NT, preferred_element_type=F32)
            g_buf[ch] = lax.dot_general(chunk_of(js, 1), d8[...], NT, preferred_element_type=F32)
            key_pos = (block0 + ch * PER_CHUNK) * HALF + lax.broadcasted_iota(jnp.int32, (CHUNK, 128), 0)
            bias = jnp.where((key_pos >= query_start) & (key_pos <= query_pos), 0.0, HIDDEN)
            s = s * (SCALE * LOG2E) + jnp.concatenate([bias] * (QCOLS // 128), axis=1)
            s_buf[ch] = s
            return jnp.maximum(top, jnp.max(s.reshape(CHUNK // 8, 8, QCOLS), axis=0))

        top = lax.fori_loop(0, chunks, score, jnp.full((8, QCOLS), HIDDEN, F32))
        top = jnp.max(top, axis=0, keepdims=True)

        def weigh(ch, carry):
            total, dot = carry
            p = jnp.exp2(s_buf[ch] - top)
            s_buf[ch] = p
            total = total + jnp.sum(p.reshape(CHUNK // 8, 8, QCOLS), axis=0)
            dot = dot + jnp.sum((p * g_buf[ch]).reshape(CHUNK // 8, 8, QCOLS), axis=0)
            return total, dot

        zeros = jnp.zeros((8, QCOLS), F32)
        total, dot = lax.fori_loop(0, chunks, weigh, (zeros, zeros))
        inverse = 1.0 / jnp.sum(total, axis=0, keepdims=True)
        delta = jnp.sum(dot, axis=0, keepdims=True) * inverse
        dq_acc[...] = jnp.zeros((HD, QCOLS), F32)

        def grads(ch, carry):
            js = places(ch)
            p = s_buf[ch] * inverse
            ds = (p * (g_buf[ch] - delta)).astype(BF16)
            dk = jnp.dot(ds, q8[...], preferred_element_type=F32)
            dv = jnp.dot(p.astype(BF16), d8[...], preferred_element_type=F32)
            dq_acc[...] += lax.dot_general(chunk_of(js, 0), ds, TN, preferred_element_type=F32)
            for t, j in enumerate(js):
                acc[j, 0] += dk[t * HALF : (t + 1) * HALF]
                acc[j, 1] += dv[t * HALF : (t + 1) * HALF]
            return carry

        lax.fori_loop(0, chunks, grads, 0)
        dq = (dq_acc[...] * SCALE).T
        for h in range(HEADS):
            dq_ref[0, half * HALF : (half + 1) * HALF, h * HD : (h + 1) * HD] = dq[h * HALF : (h + 1) * HALF].astype(BF16)

    def write(i, carry):
        for part in range(2):
            rows = slice(part * HALF, (part + 1) * HALF)
            part_ref[i % NC, i // (NZL * NC), (i // NC) % NZL, 0, rows] = (acc[2 * i + part, 0] * SCALE).astype(BF16)
            part_ref[i % NC, i // (NZL * NC), (i // NC) % NZL, 1, rows] = acc[2 * i + part, 1].astype(BF16)
        return carry

    lax.fori_loop(0, NCTX, write, 0)


def reduce_kernel(
    part_ref, xt_ref, kg_ref, vg_ref, wg_ref,
    mine, theirs, y_in, z_out, z_in, g_buf, x_buf, p_out, p_in, w_acc, w_out, w_in,
    local, a_s, a_r, c_s, c_r, y_s, y_r, z_s, z_r, g_s, g_r, p_s, p_r, w_s, w_r,
):
    x, zh, y, zl, c = place()
    slot = x * NC + c
    zz = zh * NZL + zl
    sibling = device(x, zh, y, zl, 1 - c)

    def xc_device(t):
        return device(t // NC, zh, y, zl, t % NC)

    xc_to = [(slot + o) % XC for o in range(1, XC)]
    xc_from = [(slot - o + XC) % XC for o in range(1, XC)]
    xc_peers = [xc_device(t) for t in xc_to]
    y_to = [(y + o) % NY for o in range(1, NY)]
    y_peers = [device(x, zh, t, zl, c) for t in y_to]
    z_to = [(zl + o) % NZL for o in range(1, NZL)]
    z_peers = [device(x, zh, y, t, c) for t in z_to]
    zz_to = [(zz + o) % (NZH * NZL) for o in range(1, NZH * NZL)]
    zz_peers = [device(x, t // NZL, y, t % NZL, c) for t in zz_to]
    keep = pltpu.make_async_copy(part_ref.at[c], mine, local.at[0])
    keep.start()
    keep_x = pltpu.make_async_copy(xt_ref.at[slot], x_buf.at[slot], local.at[1])
    keep_x.start()
    greet(xc_peers + y_peers + zz_peers)
    sends = []

    def go(src, dst, send, recv, to):
        copy = remote(src, dst, send, recv, to)
        copy.start()
        sends.append(copy)

    y_order = [2, 1, 3, 0]
    for o in y_order:
        t = (y + o) % NY
        go(part_ref.at[1 - c, t], theirs.at[t], c_s.at[o], c_r.at[o], sibling)
    for o in (4, 2, 6, 3, 5, 1, 7):
        go(xt_ref.at[xc_to[o - 1]], x_buf.at[slot], a_s.at[o - 1], a_r.at[o - 1], xc_peers[o - 1])
    keep.wait()

    z_order = [2, 1, 3, 0]
    for o in y_order:
        t = (y + o) % NY
        remote(part_ref.at[1 - c, t], theirs.at[t], c_s.at[o], c_r.at[o], sibling).wait_recv()
        for oz in z_order:
            tz = (zl + oz) % NZL
            mine[t, tz] = (mine[t, tz].astype(F32) + theirs[t, tz].astype(F32)).astype(BF16)
            if o:
                go(mine.at[t, tz], y_in.at[o - 1, oz], y_s.at[o - 1, oz], y_r.at[o - 1, oz], y_peers[o - 1])

    own = None
    for oz in z_order:
        tz = (zl + oz) % NZL
        total = mine[y, tz].astype(F32)
        for o in (1, 3, 2):
            remote(mine.at[y, tz], y_in.at[o - 1, oz], y_s.at[o - 1, oz], y_r.at[o - 1, oz], y_peers[o - 1]).wait_recv()
            total = total + y_in[o - 1, oz].astype(F32)
        if oz:
            z_out[oz - 1] = total.astype(BF16)
            go(z_out.at[oz - 1], z_in.at[oz - 1], z_s.at[oz - 1], z_r.at[oz - 1], z_peers[oz - 1])
        else:
            own = total
    for oz in (1, 3, 2):
        remote(z_out.at[oz - 1], z_in.at[oz - 1], z_s.at[oz - 1], z_r.at[oz - 1], z_peers[oz - 1]).wait_recv()
        own = own + z_in[oz - 1].astype(F32)
    rounded = own.astype(BF16)
    g_buf[slot, :, :HD] = rounded[0]
    g_buf[slot, :, HD:] = rounded[1]
    for o in (4, 2, 6, 3, 5, 1, 7):
        go(g_buf.at[slot], g_buf.at[slot], g_s.at[o - 1], g_r.at[o - 1], xc_peers[o - 1])
    kg_ref[0] = rounded[0]
    vg_ref[0] = rounded[1]

    keep_x.wait()
    for o in (1, 7, 2, 3, 5, 6, 4):
        t = xc_from[o - 1]
        remote(xt_ref.at[t], x_buf.at[t], a_s.at[o - 1], a_r.at[o - 1], xc_peers[o - 1]).wait_recv()
    for o in (1, 7, 2, 3, 5, 6, 4):
        t = xc_from[o - 1]
        remote(g_buf.at[t], g_buf.at[t], g_s.at[o - 1], g_r.at[o - 1], xc_peers[o - 1]).wait_recv()
    grads = jnp.concatenate([g_buf[t] for t in range(XC)], axis=0)
    own = None
    for o in y_order:
        t = (y + o) % NY
        rows = pl.ds(pl.multiple_of(t * 256, 256), 256)
        left = jnp.concatenate([x_buf[i, rows, :] for i in range(XC)], axis=1)
        term = jnp.dot(left, grads, preferred_element_type=F32)
        if o:
            p_out[o - 1] = term.astype(BF16)
            go(p_out.at[o - 1], p_in.at[o - 1], p_s.at[o - 1], p_r.at[o - 1], y_peers[o - 1])
        else:
            own = term
    for o in (1, 3, 2):
        remote(p_out.at[o - 1], p_in.at[o - 1], p_s.at[o - 1], p_r.at[o - 1], y_peers[o - 1]).wait_recv()
        own = own + p_in[o - 1].astype(F32)
    w_acc[...] = own.reshape(NZL * NZH, 32, 2 * HD)
    w_out[...] = own.reshape(NZL * NZH, 32, 2 * HD).astype(BF16)
    for o in (4, 3, 5, 2, 6, 1, 7):
        t = zz_to[o - 1]
        go(w_out.at[(t % NZL) * NZH + t // NZL], w_in.at[o - 1], w_s.at[o - 1], w_r.at[o - 1], zz_peers[o - 1])
    total = w_acc[zl * NZH + zh]
    for o in (1, 7, 2, 6, 3, 5, 4):
        remote(w_out.at[0], w_in.at[o - 1], w_s.at[o - 1], w_r.at[o - 1], zz_peers[o - 1]).wait_recv()
        total = total + w_in[o - 1].astype(F32)
    wg_ref[0] = total * (1.0 / math.sqrt(8 * SEQ))
    for copy in sends:
        copy.wait_send()


def per_device(layer_input, queries, keys, values, d_out, doc_lengths, block_order):
    vmem = pl.BlockSpec(memory_space=pltpu.VMEM)
    smem = pl.BlockSpec(memory_space=pltpu.SMEM)
    hbm = pl.BlockSpec(memory_space=pl.ANY)
    dma = pltpu.SemaphoreType.DMA
    kv, xt = pl.pallas_call(
        gather_kernel,
        out_shape=(
            jax.ShapeDtypeStruct((NCTX, 2, ROWS, HD), BF16),
            jax.ShapeDtypeStruct((XC, DCOLS, ROWS), BF16),
        ),
        in_specs=[vmem, vmem, hbm],
        out_specs=(vmem, vmem),
        scratch_shapes=[
            pltpu.VMEM((ROWS, D), BF16),
            dma(()), dma((3,)), dma((3,)), dma((4, 3)), dma((4, 3)), dma((4, 4)), dma((4, 4)),
        ],
        compiler_params=pltpu.CompilerParams(collective_id=0, has_side_effects=True, vmem_limit_bytes=32 << 20),
        name="gather_kv",
    )(keys, values, layer_input)
    dq, part = pl.pallas_call(
        attend_kernel,
        out_shape=(
            jax.ShapeDtypeStruct((1, ROWS, HEADS * HD), BF16),
            jax.ShapeDtypeStruct((NC, NY, NZL, 2, ROWS, HD), BF16),
        ),
        in_specs=[smem, smem, vmem, vmem, vmem],
        out_specs=(vmem, vmem),
        scratch_shapes=[
            pltpu.SMEM((BLOCKS,), jnp.int32),
            pltpu.VMEM((BLOCKS, 2, HALF, HD), F32),
            pltpu.VMEM((MAX_CHUNKS, CHUNK, QCOLS), F32),
            pltpu.VMEM((MAX_CHUNKS, CHUNK, QCOLS), F32),
            pltpu.VMEM((QCOLS, HD), BF16),
            pltpu.VMEM((QCOLS, HD), BF16),
            pltpu.VMEM((HD, QCOLS), F32),
        ],
        compiler_params=pltpu.CompilerParams(vmem_limit_bytes=40 << 20),
        name="attend",
    )(doc_lengths, block_order, queries, d_out, kv.reshape(NCTX, 2, 2, HALF, HD))
    kg, vg, wg = pl.pallas_call(
        reduce_kernel,
        out_shape=(
            jax.ShapeDtypeStruct((1, ROWS, HD), BF16),
            jax.ShapeDtypeStruct((1, ROWS, HD), BF16),
            jax.ShapeDtypeStruct((1, 32, 2 * HD), F32),
        ),
        in_specs=[hbm, hbm],
        out_specs=(vmem, vmem, vmem),
        scratch_shapes=[
            pltpu.VMEM((NY, NZL, 2, ROWS, HD), BF16),
            pltpu.VMEM((NY, NZL, 2, ROWS, HD), BF16),
            pltpu.VMEM((NY - 1, NZL, 2, ROWS, HD), BF16),
            pltpu.VMEM((NZL - 1, 2, ROWS, HD), BF16),
            pltpu.VMEM((NZL - 1, 2, ROWS, HD), BF16),
            pltpu.VMEM((XC, ROWS, 2 * HD), BF16),
            pltpu.VMEM((XC, DCOLS, ROWS), BF16),
            pltpu.VMEM((NY - 1, 256, 2 * HD), BF16),
            pltpu.VMEM((NY - 1, 256, 2 * HD), BF16),
            pltpu.VMEM((NZL * NZH, 32, 2 * HD), F32),
            pltpu.VMEM((NZL * NZH, 32, 2 * HD), BF16),
            pltpu.VMEM((NZL * NZH - 1, 32, 2 * HD), BF16),
            dma((2,)),
            dma((7,)), dma((7,)), dma((4,)), dma((4,)), dma((3, 4)), dma((3, 4)), dma((3,)), dma((3,)),
            dma((7,)), dma((7,)), dma((3,)), dma((3,)), dma((7,)), dma((7,)),
        ],
        compiler_params=pltpu.CompilerParams(collective_id=1, has_side_effects=True, vmem_limit_bytes=32 << 20),
        name="reduce",
    )(part, xt)
    return dq, kg, vg, wg


def solution(mesh):
    rows = P("dp", "ctx", None)
    return jax.shard_map(
        per_device,
        mesh=mesh,
        in_specs=(rows, rows, rows, rows, rows, P("dp", None), P()),
        out_specs=(rows, rows, rows, P("ctx", "dp", None)),
        check_vma=False,
    )
```

time: 638 us -> 89 us (0.14)
  waiting for transfers between devices: 506 us -> 0 us
  matrix products: 86.7 us -> 0 us
  Pallas kernels: 0 us -> 83.1 us
  between operations: 13.9 us -> 0.7 us
  local copies, waits for them, and re-layouts: 18 us -> 4.96 us
  other arithmetic: 9.99 us -> 0 us
    reduce_scatter x2 -> x0, waiting for transfers between devices: 306 us -> none  [the longest x1 160 us: per_device(): lax.psum_scatter(lax.dot_general(cols, owned, contract, precision=exact,...]
    all_gather x2 -> x0, waiting for transfers between devices: 117 us -> none  [the longest x1 59.7 us: per_device(): lax.all_gather(values[0], 'ctx', axis=0, tiled=True)]
    dot_general x57 -> x0, matrix products: 86.7 us -> none  [the longest x16 23.5 us: scores(): jnp.einsum('thd,kd->htk', q_heads, kblock, preferred_element_type=jnp.flo...]
    pallas_call x0 -> x3, Pallas kernels: none -> 83.1 us  [the longest x1 51.1 us: per_device(): pl.pallas_call(reduce_kernel, out_shape=(jax.ShapeDtypeStruct((1, ROWS, H...]
    unnamed x6 -> x0, waiting for transfers between devices: 81.6 us -> none
    dynamic_update_slice x16 -> x0, local copies, waits for them, and re-layouts: 8.25 us -> none  [per_device(): lax.scan(grad_step, jnp.zeros((local_len, heads, head_dim), jnp.float32),...]
  transfers between devices with their start and end apart: 5 -> 0, of which waited for: 5 -> 0; matrix products, arithmetic and copies ran while one was open for 1% -> 0% of each run, Pallas kernels for 0% -> 0%
where the time goes in v1:
time: 89 us; the launch traced here: 88.8 us
  Pallas kernels  83.1 us (93%)
  local copies, waits for them, and re-layouts  4.96 us (6%)
    pallas_call x1, Pallas kernels, per_device(): pl.pallas_call(reduce_kernel, out_shape=(jax.ShapeDtypeStruct((1, ROWS, H...  51.1 us
    pallas_call x1, Pallas kernels, per_device(): pl.pallas_call(gather_kernel, out_shape=(jax.ShapeDtypeStruct((NCTX, 2, R...  23.8 us
    pallas_call x1, Pallas kernels, per_device(): pl.pallas_call(attend_kernel, out_shape=(jax.ShapeDtypeStruct((1, ROWS, H...  8.27 us
    unnamed x17, local copies, waits for them, and re-layouts  4.96 us

profile of v1, /device:TPU:1, one launch (start us, length us, event | category | flops | bytes accessed | tf_op | source)
XLA Modules:
  0.0 88.8 jit_solution(9501564987589357310)
XLA Ops:
  0.6 0.0 copy-start
  0.6 1.6 %copy-done = bf16[1,128,8192]{2,1,0:T(8,128)(2,1)S(1)} copy-done((bf16[1,128,8192]{2,1,0:T(8,128)(2,1)S(1)}, bf16[1,128,8192]{2,1,0:T(8,128)(2,1)}, u32[]{:S(2)}) %copy-start) | copy-done | bytes 2097176
  2.2 0.0 copy-start.3
  2.2 0.8 copy-done.3
  3.0 0.0 copy-start.4
  3.0 0.8 copy-done.4
  3.7 0.0 copy-start.1
  3.7 0.0 copy-start.2
  3.7 0.0 copy-start.5
  3.7 0.0 copy-start.6
  3.8 23.8 %gather_kv.1 = (bf16[32,2,128,128]{3,2,1,0:T(8,128)(2,1)S(1)}, bf16[8,1024,128]{2,1,0:T(8,128)(2,1)S(1)}) custom-call(bf16[1,128,128]{2,1,0:T(8,128)(2,1)S(1)} %copy-done.3, bf16[1,128,128]{2,1,0:T(8,128)(2,1)S(1)} %copy-done.4, bf16[1,128,8192]{2,1,0:T(8,128)(2,1)S(1)} %copy-done), custom_call_target="tpu_custom_call" | custom-call | tf_op jit(solution)/shard_map/gather_kv/pallas_call | solution.py:336
  27.6 0.0 copy-done.1
  27.6 0.0 copy-done.2
  27.6 0.0 copy-done.5
  27.6 0.0 copy-done.6
  27.6 8.3 %attend.1 = (bf16[1,128,1024]{2,1,0:T(8,128)(2,1)}, bf16[2,4,4,2,128,128]{5,4,3,2,1,0:T(8,128)(2,1)S(1)}) custom-call(s32[1,8]{1,0:T(1,128)S(1)} %copy-done.5, s32[64]{0:T(128)S(1)} %copy-done.6, bf16[1,128,1024]{2,1,0:T(8,128)(2,1)S(1)} %copy-done.1, bf16[1,128,1024]{2,1,0:T(8,128)(2,1)S(1)} %copy-done.2, bf16[32,2,2,64,128]{4,3,2,1,0:T(8,128)(2,1)S(1)} %bitcast.1), custom_call_target="tpu_custom_call" | custom-call | tf_op jit(solution)/shard_map/attend/pallas_call | solution.py:351
  35.9 51.1 %reduce.1 = (bf16[1,128,128]{2,1,0:T(8,128)(2,1)S(1)}, bf16[1,128,128]{2,1,0:T(8,128)(2,1)S(1)}, f32[1,32,256]{2,1,0:T(8,128)S(1)}) custom-call(bf16[2,4,4,2,128,128]{5,4,3,2,1,0:T(8,128)(2,1)S(1)} %get-tuple-element.13.part_ref, bf16[8,1024,128]{2,1,0:T(8,128)(2,1)S(1)} %get-tuple-element.14.xt_ref), custom_call_target="tpu_custom_call" | custom-call | tf_op jit(solution)/shard_map/reduce/pallas_call | solution.py:371
  86.9 0.6 copy.14
  87.6 0.6 copy.15
  88.2 0.6 copy.16
Async XLA Ops:
  0.6 1.6 %copy-start = (bf16[1,128,8192]{2,1,0:T(8,128)(2,1)S(1)}, bf16[1,128,8192]{2,1,0:T(8,128)(2,1)}, u32[]{:S(2)}) copy-start(bf16[1,128,8192]{2,1,0:T(8,128)(2,1)} %x_hbm.1) | copy-start | bytes 6291460
  2.2 0.8 copy-start.3
  3.0 0.8 copy-start.4
  3.7 23.8 %copy-start.1 = (bf16[1,128,1024]{2,1,0:T(8,128)(2,1)S(1)}, bf16[1,128,1024]{2,1,0:T(8,128)(2,1)}, u32[]{:S(2)}) copy-start(bf16[1,128,1024]{2,1,0:T(8,128)(2,1)} %q_ref.1) | copy-start | bytes 786436
  3.7 23.8 %copy-start.2 = (bf16[1,128,1024]{2,1,0:T(8,128)(2,1)S(1)}, bf16[1,128,1024]{2,1,0:T(8,128)(2,1)}, u32[]{:S(2)}) copy-start(bf16[1,128,1024]{2,1,0:T(8,128)(2,1)} %d_ref.1) | copy-start | bytes 786436
  3.7 23.8 %copy-start.5 = (s32[1,8]{1,0:T(1,128)S(1)}, s32[1,8]{1,0:T(1,128)}, u32[]{:S(2)}) copy-start(s32[1,8]{1,0:T(1,128)} %doc_ref.1) | copy-start | bytes 100
  3.7 23.9 %copy-start.6 = (s32[64]{0:T(128)S(1)}, s32[64]{0:T(128)}, u32[]{:S(2)}) copy-start(s32[64]{0:T(128)} %order_ref.1) | copy-start | bytes 772

commit v2 on v0

v2 whole, which is shorter than its diff:
```python
import math

import jax
import jax.numpy as jnp
from jax import lax
from jax.experimental import pallas as pl
from jax.experimental.pallas import tpu as pltpu
from jax.sharding import PartitionSpec as P

NX, NY, NZL, NZH, NC = 4, 4, 4, 2, 2
NCTX = NY * NZL * NC
ROWS = 128
HD = 128
HEADS = 8
HALF = 64
BLOCKS = 64
SEQ = 4096
D = 8192
NDOCS = 8
XC = NX * NC
DCOLS = D // XC
WINDOW = 17
STEP = 4
QCOLS = HEADS * HALF
SCALE = 1.0 / math.sqrt(HD)
LOG2E = math.log2(math.e)
HIDDEN = -1e30
MESH = pl.DeviceIdType.MESH
F32 = jnp.float32
BF16 = jnp.bfloat16
NT = (((1,), (1,)), ((), ()))
TN = (((0,), (0,)), ((), ()))


def place():
    dp = lax.axis_index("dp")
    ctx = lax.axis_index("ctx")
    return dp // NZH, dp % NZH, ctx // (NZL * NC), (ctx // NC) % NZL, ctx % NC


def device(x, zh, y, zl, c):
    return (x * NZH + zh, (y * NZL + zl) * NC + c)


def remote(src, dst, send, recv, to):
    return pltpu.make_async_remote_copy(
        src_ref=src, dst_ref=dst, send_sem=send, recv_sem=recv, device_id=to, device_id_type=MESH
    )


def greet(peers):
    barrier = pltpu.get_barrier_semaphore()
    for peer in peers:
        pl.semaphore_signal(barrier, inc=1, device_id=peer, device_id_type=MESH)
    pl.semaphore_wait(barrier, len(peers))


def kernel(
    doc_ref, order_ref, order_row, k_hbm, v_hbm, x_hbm, q_hbm, d_hbm, dq_ref, kg_ref, vg_ref, wg_ref,
    stored, stored_v, k_all, v_all, xv, xt, x_in, q_in, d_in, q8, d8, p_buf, g_buf, ds_buf, acc, part,
    theirs, y_in, z_out, z_in, g_all, p_out, p_in, w_acc, w_out, w_in, local,
    gz_s, gz_r, gy_s, gy_r, gc_s, gc_r, a_s, a_r, c_s, c_r, y_s, y_r, z_s, z_r, g_s, g_r, p_s, p_r, w_s, w_r,
):
    x, zh, y, zl, c = place()
    kv = (k_all, v_all)
    slot = x * NC + c
    zz = zh * NZL + zl

    def rank(q, p, core):
        return (((y - q + NY) % NY) * NZL + (zl - p + NZL) % NZL) * NC + core

    me = rank(0, 0, c)
    loads = [
        pltpu.make_async_copy(k_hbm.at[0, pl.ds(0, HALF)], kv[0].at[me, 0], local.at[0]),
        pltpu.make_async_copy(k_hbm.at[0, pl.ds(HALF, HALF)], kv[0].at[me, 1], local.at[1]),
        pltpu.make_async_copy(v_hbm.at[0, pl.ds(0, HALF)], kv[1].at[me, 0], local.at[2]),
        pltpu.make_async_copy(v_hbm.at[0, pl.ds(HALF, HALF)], kv[1].at[me, 1], local.at[3]),
        pltpu.make_async_copy(x_hbm.at[0], xv, local.at[4]),
        pltpu.make_async_copy(q_hbm.at[0], q_in, local.at[5]),
        pltpu.make_async_copy(d_hbm.at[0], d_in, local.at[6]),
    ]
    for load in loads:
        load.start()

    sibling = device(x, zh, y, zl, 1 - c)
    y_peers = [device(x, zh, (y + o) % NY, zl, c) for o in range(1, NY)]
    z_peers = [device(x, zh, y, (zl + o) % NZL, c) for o in range(1, NZL)]
    xc_to = [(slot + o) % XC for o in range(1, XC)]
    xc_from = [(slot - o + XC) % XC for o in range(1, XC)]
    xc_peers = [device(t // NC, zh, y, zl, t % NC) for t in xc_to]
    zz_to = [(zz + o) % (NZH * NZL) for o in range(1, NZH * NZL)]
    zz_peers = [device(x, t // NZL, y, t % NZL, c) for t in zz_to]
    greet(xc_peers + y_peers + zz_peers)
    sends = []

    def go(src, dst, send, recv, to):
        copy = remote(src, dst, send, recv, to)
        copy.start()
        sends.append(copy)

    def arrived(dst, send, recv, to):
        remote(dst, dst, send, recv, to).wait_recv()

    Y = (2, 1, 3)
    Z = (2, 1, 3)
    XS = (4, 2, 6, 3, 5, 1, 7)
    XR = (1, 7, 2, 3, 5, 6, 4)

    def to_z(w):
        for o in Z:
            go(kv[w].at[me], kv[w].at[me], gz_s.at[w, o - 1], gz_r.at[w, o - 1], z_peers[o - 1])

    def to_y(w, p):
        r = rank(0, p, c)
        for o in Y:
            go(kv[w].at[r], kv[w].at[r], gy_s.at[w, p, o - 1], gy_r.at[w, p, o - 1], y_peers[o - 1])

    def to_core(w, q, p):
        r = rank(q, p, c)
        go(kv[w].at[r], kv[w].at[r], gc_s.at[w, q, p], gc_r.at[w, q, p], sibling)

    def from_z(w, p):
        arrived(kv[w].at[rank(0, p, c)], gz_s.at[w, p - 1], gz_r.at[w, p - 1], z_peers[p - 1])

    def from_y(w, q, p):
        arrived(kv[w].at[rank(q, p, c)], gy_s.at[w, p, q - 1], gy_r.at[w, p, q - 1], y_peers[q - 1])

    def from_core(w):
        for p in range(NZL):
            for q in range(NY):
                arrived(kv[w].at[rank(q, p, 1 - c)], gc_s.at[w, q, p], gc_r.at[w, q, p], sibling)

    loads[0].wait()
    loads[1].wait()
    to_z(0)
    to_y(0, 0)
    to_core(0, 0, 0)
    loads[2].wait()
    loads[3].wait()
    to_z(1)
    to_core(1, 0, 0)

    same = order_row[...] == lax.broadcasted_iota(jnp.int32, (BLOCKS, BLOCKS), 0)
    column = lax.broadcasted_iota(jnp.int32, (BLOCKS, BLOCKS), 1)
    found = jnp.max(jnp.where(same, column, 0), axis=1, keepdims=True)
    stored_v[...] = jnp.broadcast_to(found, (BLOCKS, 128))
    load_stored = pltpu.make_async_copy(stored_v, stored, local.at[7])
    load_stored.start()

    to_row = lax.broadcasted_iota(jnp.int32, (256, 256), 0)
    from_row = lax.broadcasted_iota(jnp.int32, (256, 256), 1)
    group = to_row // 64
    source = (group % 2) * 128 + (group // 2) * 64 + to_row % 64
    pick = jnp.where(source == from_row, 1.0, 0.0).astype(BF16)

    def turn(core, xh):
        for k in range(NY * NZL // 2):
            at = 2 * k * 512 + core * 256 + xh * 128
            pair = jnp.concatenate([xv[:, at : at + 128], xv[:, at + 512 : at + 640]], axis=1)
            turned = lax.dot_general(pick, pair, NT, preferred_element_type=F32).astype(BF16)
            xt[(2 * xh) * NC + core, k * 128 : (k + 1) * 128, :] = turned[:128]
            xt[(2 * xh + 1) * NC + core, k * 128 : (k + 1) * 128, :] = turned[128:]

    loads[4].wait()
    turn(0, 0)
    for p in (1, 3, 2):
        from_z(0, p)
        to_y(0, p)
        to_core(0, 0, p)
    turn(0, 1)
    turn(1, 0)
    turn(1, 1)
    keep_x = pltpu.make_async_copy(xt.at[slot], x_in.at[slot], local.at[4])
    keep_x.start()
    for o in XS:
        go(xt.at[xc_to[o - 1]], x_in.at[slot], a_s.at[o - 1], a_r.at[o - 1], xc_peers[o - 1])
    to_y(1, 0)
    for p in (1, 3, 2):
        from_z(1, p)
        to_y(1, p)
        to_core(1, 0, p)
    for w in range(2):
        for half in range(2):
            acc[w, half, 0] = jnp.zeros((HALF, HD), F32)
            acc[w, half, WINDOW + 1] = jnp.zeros((HALF, HD), F32)
    loads[5].wait()
    loads[6].wait()
    for half in range(2):
        for h in range(HEADS):
            q8[half, h * HALF : (h + 1) * HALF, :] = q_in[half * HALF : (half + 1) * HALF, h * HD : (h + 1) * HD]
            d8[half, h * HALF : (h + 1) * HALF, :] = d_in[half * HALF : (half + 1) * HALF, h * HD : (h + 1) * HD]
    load_stored.wait()
    ends = []
    end = 0
    for i in range(NDOCS):
        end = end + doc_ref[0, i]
        ends.append(end)
    blocks = [order_ref[2 * me + half] for half in range(2)]
    for p in (0, 1, 3, 2):
        for q in (1, 3, 2):
            from_y(0, q, p)
            to_core(0, q, p)
    from_core(0)

    def each_step(step, carry):
        def body(i, carry):
            return step(i * STEP, STEP, pl.ds(pl.multiple_of(i * (STEP * HALF), STEP * HALF), STEP * HALF), carry)

        carry = lax.fori_loop(0, WINDOW // STEP, body, carry)
        return step(WINDOW - 1, 1, pl.ds((WINDOW - 1) * HALF, HALF), carry)

    def window(w, half, t, count):
        at = [jnp.clip(blocks[half] - (WINDOW - 1) + t + i, 0, BLOCKS - 1) for i in range(count)]
        js = [jnp.clip(stored[i, 0], 0, BLOCKS - 1) for i in at]
        return jnp.concatenate([kv[w][j // 2, j % 2] for j in js], axis=0)

    def fold(a):
        return a.reshape(a.shape[0] // 8, 8, QCOLS)

    def softmax(half):
        lane = lax.broadcasted_iota(jnp.int32, (1, 128), 1)
        query_pos = blocks[half] * HALF + lane % HALF
        query_start = jnp.zeros((1, 128), jnp.int32)
        for end in ends:
            query_start = jnp.where(end <= query_pos, end, query_start)

        def score(t, count, rows, top):
            s = lax.dot_general(window(0, half, t, count), q8[half], NT, preferred_element_type=F32)
            key_pos = (blocks[half] - (WINDOW - 1) + t) * HALF + lax.broadcasted_iota(jnp.int32, (count * HALF, 128), 0)
            bias = jnp.where((key_pos >= query_start) & (key_pos <= query_pos), 0.0, HIDDEN)
            s = s * (SCALE * LOG2E) + jnp.concatenate([bias] * (QCOLS // 128), axis=1)
            p_buf[half, rows] = s
            return jnp.maximum(top, jnp.max(fold(s), axis=0))

        top = each_step(score, jnp.full((8, QCOLS), HIDDEN, F32))
        top = jnp.max(top, axis=0, keepdims=True)

        def weigh(t, count, rows, total):
            p = jnp.exp2(p_buf[half, rows] - top)
            p_buf[half, rows] = p
            return total + jnp.sum(fold(p), axis=0)

        total = each_step(weigh, jnp.zeros((8, QCOLS), F32))
        inverse = 1.0 / jnp.sum(total, axis=0, keepdims=True)

        def value_terms(t, count, rows, carry):
            pb = (p_buf[half, rows] * inverse).astype(BF16)
            dv = jnp.dot(pb, d8[half], preferred_element_type=F32)
            acc[1, half, pl.ds(1 + t, count)] = dv.reshape(count, HALF, HD)
            return carry

        each_step(value_terms, 0)
        return inverse

    def key_terms(half, inverse):
        def prob_grads(t, count, rows, dot):
            g = lax.dot_general(window(1, half, t, count), d8[half], NT, preferred_element_type=F32)
            g_buf[rows] = g
            return dot + jnp.sum(fold(p_buf[half, rows] * g), axis=0)

        dot = each_step(prob_grads, jnp.zeros((8, QCOLS), F32))
        delta = jnp.sum(dot, axis=0, keepdims=True) * inverse

        def terms(t, count, rows, carry):
            ds = (p_buf[half, rows] * inverse * (g_buf[rows] - delta)).astype(BF16)
            ds_buf[half, rows] = ds
            dk = jnp.dot(ds, q8[half], preferred_element_type=F32) * SCALE
            acc[0, half, pl.ds(1 + t, count)] = dk.reshape(count, HALF, HD)
            return carry

        each_step(terms, 0)

    def query_terms(half):
        def terms(t, count, rows, total):
            return total + lax.dot_general(window(0, half, t, count), ds_buf[half, rows], TN, preferred_element_type=F32)

        dq = (each_step(terms, jnp.zeros((HD, QCOLS), F32)) * SCALE).T
        for h in range(HEADS):
            dq_ref[0, half * HALF : (half + 1) * HALF, h * HD : (h + 1) * HD] = dq[h * HALF : (h + 1) * HALF].astype(BF16)

    def in_stored_order(w, core, t):
        def body(i, carry):
            for part_half in range(2):
                block = order_ref[2 * ((t * NZL + i) * NC + core) + part_half]
                both = [acc[w, h, jnp.clip(block - blocks[h] + WINDOW, 0, WINDOW + 1)] for h in range(2)]
                part[w, core, t, i, part_half * HALF : (part_half + 1) * HALF] = (both[0] + both[1]).astype(BF16)
            return carry

        lax.fori_loop(0, NZL, body, 0)

    def sum_to_core(w):
        for o in (2, 1, 3, 0):
            t = (y + o) % NY
            in_stored_order(w, 1 - c, t)
            go(part.at[w, 1 - c, t], theirs.at[w, t], c_s.at[w, o], c_r.at[w, o], sibling)
        for o in (2, 1, 3, 0):
            in_stored_order(w, c, (y + o) % NY)

    def sum_to_y(w):
        for o in (2, 1, 3, 0):
            t = (y + o) % NY
            arrived(theirs.at[w, t], c_s.at[w, o], c_r.at[w, o], sibling)
            for oz in (2, 1, 3, 0):
                tz = (zl + oz) % NZL
                part[w, c, t, tz] = (part[w, c, t, tz].astype(F32) + theirs[w, t, tz].astype(F32)).astype(BF16)
                if o:
                    go(part.at[w, c, t, tz], y_in.at[w, o - 1, oz], y_s.at[w, o - 1, oz], y_r.at[w, o - 1, oz], y_peers[o - 1])

    def sum_to_z(w):
        for oz in (2, 1, 3, 0):
            total = part[w, c, y, (zl + oz) % NZL].astype(F32)
            for o in (1, 3, 2):
                arrived(y_in.at[w, o - 1, oz], y_s.at[w, o - 1, oz], y_r.at[w, o - 1, oz], y_peers[o - 1])
                total = total + y_in[w, o - 1, oz].astype(F32)
            if oz:
                z_out[w, oz - 1] = total.astype(BF16)
                go(z_out.at[w, oz - 1], z_in.at[w, oz - 1], z_s.at[w, oz - 1], z_r.at[w, oz - 1], z_peers[oz - 1])
        return total

    def sum_to_x(w, total, out_ref):
        for oz in (1, 3, 2):
            arrived(z_in.at[w, oz - 1], z_s.at[w, oz - 1], z_r.at[w, oz - 1], z_peers[oz - 1])
            total = total + z_in[w, oz - 1].astype(F32)
        rounded = total.astype(BF16)
        g_all[w, slot] = rounded
        for o in XS:
            go(g_all.at[w, slot], g_all.at[w, slot], g_s.at[w, o - 1], g_r.at[w, o - 1], xc_peers[o - 1])
        out_ref[0] = rounded

    def product(w):
        for o in XR:
            t = xc_from[o - 1]
            arrived(g_all.at[w, t], g_s.at[w, o - 1], g_r.at[w, o - 1], xc_peers[o - 1])
        right = jnp.concatenate([g_all[w, t] for t in range(XC)], axis=0)
        for o in (2, 1, 3, 0):
            rows = pl.ds(pl.multiple_of(((y + o) % NY) * 256, 256), 256)
            left = jnp.concatenate([x_in[i, rows, :] for i in range(XC)], axis=1)
            term = jnp.dot(left, right, preferred_element_type=F32)
            if o:
                p_out[w, o - 1] = term.astype(BF16)
                go(p_out.at[w, o - 1], p_in.at[w, o - 1], p_s.at[w, o - 1], p_r.at[w, o - 1], y_peers[o - 1])
        w_acc[w] = term.reshape(NZL * NZH, 32, HD)

    def product_to_z(w):
        for o in (1, 3, 2):
            arrived(p_in.at[w, o - 1], p_s.at[w, o - 1], p_r.at[w, o - 1], y_peers[o - 1])
        total = w_acc[w].reshape(256, HD) + p_in[w, 0].astype(F32) + p_in[w, 1].astype(F32) + p_in[w, 2].astype(F32)
        w_acc[w] = total.reshape(NZL * NZH, 32, HD)
        w_out[w] = total.reshape(NZL * NZH, 32, HD).astype(BF16)
        for o in (4, 3, 5, 2, 6, 1, 7):
            t = zz_to[o - 1]
            go(w_out.at[w, (t % NZL) * NZH + t // NZL], w_in.at[w, o - 1], w_s.at[w, o - 1], w_r.at[w, o - 1], zz_peers[o - 1])

    def finish(w):
        total = w_acc[w, zl * NZH + zh]
        for o in (1, 7, 2, 6, 3, 5, 4):
            arrived(w_in.at[w, o - 1], w_s.at[w, o - 1], w_r.at[w, o - 1], zz_peers[o - 1])
            total = total + w_in[w, o - 1].astype(F32)
        wg_ref[0, :, w * HD : (w + 1) * HD] = total * (1.0 / math.sqrt(8 * SEQ))

    inverses = [softmax(half) for half in range(2)]
    sum_to_core(1)
    for p in (0, 1, 3, 2):
        for q in (1, 3, 2):
            from_y(1, q, p)
            to_core(1, q, p)
    sum_to_y(1)
    from_core(1)
    for half in range(2):
        key_terms(half, inverses[half])
    sum_to_core(0)
    v_total = sum_to_z(1)
    sum_to_y(0)
    sum_to_x(1, v_total, vg_ref)
    for half in range(2):
        query_terms(half)
    k_total = sum_to_z(0)
    keep_x.wait()
    for o in XR:
        t = xc_from[o - 1]
        arrived(x_in.at[t], a_s.at[o - 1], a_r.at[o - 1], xc_peers[o - 1])
    product(1)
    sum_to_x(0, k_total, kg_ref)
    product_to_z(1)
    product(0)
    finish(1)
    product_to_z(0)
    finish(0)
    for copy in sends:
        copy.wait_send()


def per_device(layer_input, queries, keys, values, d_out, doc_lengths, block_order):
    vmem = pl.BlockSpec(memory_space=pltpu.VMEM)
    smem = pl.BlockSpec(memory_space=pltpu.SMEM)
    hbm = pl.BlockSpec(memory_space=pltpu.HBM)

    def dma(*shape):
        return [pltpu.SemaphoreType.DMA(shape)] * 2

    def buf(*shape, dtype=BF16):
        return pltpu.VMEM(shape, dtype)

    operands = (doc_lengths, block_order, block_order.reshape(1, BLOCKS), keys, values, layer_input, queries, d_out)
    dq, kg, vg, wg = pl.pallas_call(
        kernel,
        out_shape=(
            jax.ShapeDtypeStruct((1, ROWS, HEADS * HD), BF16),
            jax.ShapeDtypeStruct((1, ROWS, HD), BF16),
            jax.ShapeDtypeStruct((1, ROWS, HD), BF16),
            jax.ShapeDtypeStruct((1, 32, 2 * HD), F32),
        ),
        in_specs=[smem, smem, vmem, hbm, hbm, hbm, hbm, hbm],
        out_specs=(vmem, vmem, vmem, vmem),
        scratch_shapes=[
            pltpu.SMEM((BLOCKS, 128), jnp.int32),
            buf(BLOCKS, 128, dtype=jnp.int32),
            buf(NCTX, 2, HALF, HD),
            buf(NCTX, 2, HALF, HD),
            buf(ROWS, D),
            buf(XC, DCOLS, ROWS),
            buf(XC, DCOLS, ROWS),
            buf(ROWS, HEADS * HD),
            buf(ROWS, HEADS * HD),
            buf(2, QCOLS, HD),
            buf(2, QCOLS, HD),
            buf(2, WINDOW * HALF, QCOLS, dtype=F32),
            buf(WINDOW * HALF, QCOLS, dtype=F32),
            buf(2, WINDOW * HALF, QCOLS),
            buf(2, 2, WINDOW + 2, HALF, HD, dtype=F32),
            buf(2, NC, NY, NZL, ROWS, HD),
            buf(2, NY, NZL, ROWS, HD),
            buf(2, NY - 1, NZL, ROWS, HD),
            buf(2, NZL - 1, ROWS, HD),
            buf(2, NZL - 1, ROWS, HD),
            buf(2, XC, ROWS, HD),
            buf(2, NY - 1, 256, HD),
            buf(2, NY - 1, 256, HD),
            buf(2, NZL * NZH, 32, HD, dtype=F32),
            buf(2, NZL * NZH, 32, HD),
            buf(2, NZL * NZH - 1, 32, HD),
            pltpu.SemaphoreType.DMA((8,)),
            *dma(2, 3), *dma(2, 4, 3), *dma(2, 4, 4), *dma(7), *dma(2, 4), *dma(2, 3, 4), *dma(2, 3),
            *dma(2, 7), *dma(2, 3), *dma(2, 7),
        ],
        compiler_params=pltpu.CompilerParams(collective_id=0, has_side_effects=True, vmem_limit_bytes=48 << 20),
        name="backward",
    )(*(pltpu.with_memory_space_constraint(a, pltpu.HBM) for a in operands))
    return dq, kg, vg, wg


def solution(mesh):
    rows = P("dp", "ctx", None)
    return jax.shard_map(
        per_device,
        mesh=mesh,
        in_specs=(rows, rows, rows, rows, rows, P("dp", None), P()),
        out_specs=(rows, rows, rows, P("ctx", "dp", None)),
        check_vma=False,
    )
```

time: 638 us -> 70 us (0.11)
  waiting for transfers between devices: 506 us -> 0 us
  matrix products: 86.7 us -> 0 us
  Pallas kernels: 0 us -> 66.7 us
  local copies, waits for them, and re-layouts: 18 us -> 2.55 us
  between operations: 13.9 us -> 0.64 us
  other arithmetic: 9.99 us -> 0 us
    reduce_scatter x2 -> x0, waiting for transfers between devices: 306 us -> none  [the longest x1 160 us: per_device(): lax.psum_scatter(lax.dot_general(cols, owned, contract, precision=exact,...]
    all_gather x2 -> x0, waiting for transfers between devices: 117 us -> none  [the longest x1 59.7 us: per_device(): lax.all_gather(values[0], 'ctx', axis=0, tiled=True)]
    dot_general x57 -> x0, matrix products: 86.7 us -> none  [the longest x16 23.5 us: scores(): jnp.einsum('thd,kd->htk', q_heads, kblock, preferred_element_type=jnp.flo...]
    unnamed x6 -> x0, waiting for transfers between devices: 81.6 us -> none
    pallas_call x0 -> x1, Pallas kernels: none -> 66.7 us  [per_device(): pl.pallas_call(kernel, out_shape=(jax.ShapeDtypeStruct((1, ROWS, HEADS *...]
    dynamic_update_slice x16 -> x0, local copies, waits for them, and re-layouts: 8.25 us -> none  [per_device(): lax.scan(grad_step, jnp.zeros((local_len, heads, head_dim), jnp.float32),...]
  transfers between devices with their start and end apart: 5 -> 0, of which waited for: 5 -> 0; matrix products, arithmetic and copies ran while one was open for 1% -> 0% of each run, Pallas kernels for 0% -> 0%
where the time goes in v2:
time: 70 us; the launch traced here: 69.9 us
  Pallas kernels  66.7 us (95%)
  local copies, waits for them, and re-layouts  2.55 us (4%)
    pallas_call x1, Pallas kernels, per_device(): pl.pallas_call(kernel, out_shape=(jax.ShapeDtypeStruct((1, ROWS, HEADS *...  66.7 us
    unnamed x4, local copies, waits for them, and re-layouts  2.55 us

profile of v2, /device:TPU:1, one launch (start us, length us, event | category | flops | bytes accessed | tf_op | source)
XLA Modules:
  0.0 69.9 jit_solution(15913602782443033577)
XLA Ops:
  0.6 66.7 %backward.1 = (bf16[1,128,1024]{2,1,0:T(8,128)(2,1)S(1)}, bf16[1,128,128]{2,1,0:T(8,128)(2,1)S(1)}, bf16[1,128,128]{2,1,0:T(8,128)(2,1)S(1)}, f32[1,32,256]{2,1,0:T(8,128)S(1)}) custom-call(s32[1,8]{1,0:T(1,128)} %doc_ref.1, s32[64]{0:T(128)} %order_ref.1, s32[1,64]{1,0:T(1,128)} %bitcast.1, bf16[1,128,128]{2,1,0:T(8,128)(2,1)} %k_hbm.1, ...), custom_call_target="tpu_custom_call" | custom-call | tf_op jit(solution)/shard_map/backward/pallas_call | solution.py:405
  67.3 0.7 %copy.15 = bf16[1,128,1024]{2,1,0:T(8,128)(2,1)} copy(bf16[1,128,1024]{2,1,0:T(8,128)(2,1)S(1)} %get-tuple-element.8) | data formatting | bytes 524288
  68.1 0.6 copy.16
  68.7 0.6 copy.17
  69.3 0.6 copy.18

commit v3 on v2

--- a/solution.py
+++ b/solution.py
@@ -58,8 +58,8 @@
 def kernel(
     doc_ref, order_ref, order_row, k_hbm, v_hbm, x_hbm, q_hbm, d_hbm, dq_ref, kg_ref, vg_ref, wg_ref,
     stored, stored_v, k_all, v_all, xv, xt, x_in, q_in, d_in, q8, d8, p_buf, g_buf, ds_buf, acc, part,
-    theirs, y_in, z_out, z_in, g_all, p_out, p_in, w_acc, w_out, w_in, local,
-    gz_s, gz_r, gy_s, gy_r, gc_s, gc_r, a_s, a_r, c_s, c_r, y_s, y_r, z_s, z_r, g_s, g_r, p_s, p_r, w_s, w_r,
+    theirs, y_out, y_own, y_in, z_out, z_in, g_all, p_out, p_in, w_acc, w_out, w_in, local,
+    gz_s, gz_r, gy_s, gy_r, gh_s, gh_r, gc_s, gc_r, a_s, a_r, c_s, c_r, y_s, y_r, z_s, z_r, g_s, g_r, gs_s, gs_r, p_s, p_r, w_s, w_r,
 ):
     x, zh, y, zl, c = place()
     kv = (k_all, v_all)
@@ -88,6 +88,7 @@
     xc_to = [(slot + o) % XC for o in range(1, XC)]
     xc_from = [(slot - o + XC) % XC for o in range(1, XC)]
     xc_peers = [device(t // NC, zh, y, zl, t % NC) for t in xc_to]
+    x_peers = [device((x + o) % NX, zh, y, zl, c) for o in range(1, NX)]
     zz_to = [(zz + o) % (NZH * NZL) for o in range(1, NZH * NZL)]
     zz_peers = [device(x, t // NZL, y, t % NZL, c) for t in zz_to]
     greet(xc_peers + y_peers + zz_peers)
@@ -101,7 +102,6 @@
     def arrived(dst, send, recv, to):
         remote(dst, dst, send, recv, to).wait_recv()
 
-    Y = (2, 1, 3)
     Z = (2, 1, 3)
     XS = (4, 2, 6, 3, 5, 1, 7)
     XR = (1, 7, 2, 3, 5, 6, 4)
@@ -112,8 +112,21 @@
 
     def to_y(w, p):
         r = rank(0, p, c)
-        for o in Y:
+        for o in (1, 3):
             go(kv[w].at[r], kv[w].at[r], gy_s.at[w, p, o - 1], gy_r.at[w, p, o - 1], y_peers[o - 1])
+
+    def relay(w, p):
+        for q, half in ((1, 0), (3, 1)):
+            r = rank(q, p, c)
+            arrived(kv[w].at[r], gy_s.at[w, p, q - 1], gy_r.at[w, p, q - 1], y_peers[q - 1])
+            go(kv[w].at[r, half], kv[w].at[r, half], gh_s.at[w, p, half], gh_r.at[w, p, half], y_peers[q - 1])
+            to_core(w, q, p)
+
+    def relayed(w, p):
+        r = rank(2, p, c)
+        for q, half in ((1, 0), (3, 1)):
+            arrived(kv[w].at[r, half], gh_s.at[w, p, half], gh_r.at[w, p, half], y_peers[q - 1])
+        to_core(w, 2, p)
 
     def to_core(w, q, p):
         r = rank(q, p, c)
@@ -121,9 +134,6 @@
 
     def from_z(w, p):
         arrived(kv[w].at[rank(0, p, c)], gz_s.at[w, p - 1], gz_r.at[w, p - 1], z_peers[p - 1])
-
-    def from_y(w, q, p):
-        arrived(kv[w].at[rank(q, p, c)], gy_s.at[w, p, q - 1], gy_r.at[w, p, q - 1], y_peers[q - 1])
 
     def from_core(w):
         for p in range(NZL):
@@ -137,7 +147,7 @@
     to_core(0, 0, 0)
     loads[2].wait()
     loads[3].wait()
-    to_z(1)
+    to_y(1, 0)
     to_core(1, 0, 0)
 
     same = order_row[...] == lax.broadcasted_iota(jnp.int32, (BLOCKS, BLOCKS), 0)
@@ -163,22 +173,26 @@
 
     loads[4].wait()
     turn(0, 0)
+    turn(0, 1)
+    to_z(1)
     for p in (1, 3, 2):
         from_z(0, p)
         to_y(0, p)
         to_core(0, 0, p)
-    turn(0, 1)
+    relay(0, 0)
     turn(1, 0)
     turn(1, 1)
     keep_x = pltpu.make_async_copy(xt.at[slot], x_in.at[slot], local.at[4])
     keep_x.start()
     for o in XS:
         go(xt.at[xc_to[o - 1]], x_in.at[slot], a_s.at[o - 1], a_r.at[o - 1], xc_peers[o - 1])
-    to_y(1, 0)
+    for p in (1, 3, 2):
+        relay(0, p)
     for p in (1, 3, 2):
         from_z(1, p)
         to_y(1, p)
         to_core(1, 0, p)
+    relay(1, 0)
     for w in range(2):
         for half in range(2):
             acc[w, half, 0] = jnp.zeros((HALF, HD), F32)
@@ -197,17 +211,10 @@
         ends.append(end)
     blocks = [order_ref[2 * me + half] for half in range(2)]
     for p in (0, 1, 3, 2):
-        for q in (1, 3, 2):
-            from_y(0, q, p)
-            to_core(0, q, p)
+        relayed(0, p)
     from_core(0)
 
-    def each_step(step, carry):
-        def body(i, carry):
-            return step(i * STEP, STEP, pl.ds(pl.multiple_of(i * (STEP * HALF), STEP * HALF), STEP * HALF), carry)
-
-        carry = lax.fori_loop(0, WINDOW // STEP, body, carry)
-        return step(WINDOW - 1, 1, pl.ds((WINDOW - 1) * HALF, HALF), carry)
+    STEPS = [(t, min(STEP, WINDOW - t), slice(t * HALF, min(t + STEP, WINDOW) * HALF)) for t in range(0, WINDOW, STEP)]
 
     def window(w, half, t, count):
         at = [jnp.clip(blocks[half] - (WINDOW - 1) + t + i, 0, BLOCKS - 1) for i in range(count)]
@@ -217,98 +224,102 @@
     def fold(a):
         return a.reshape(a.shape[0] // 8, 8, QCOLS)
 
-    def softmax(half):
-        lane = lax.broadcasted_iota(jnp.int32, (1, 128), 1)
-        query_pos = blocks[half] * HALF + lane % HALF
+    def query_span(half):
+        query_pos = blocks[half] * HALF + lax.broadcasted_iota(jnp.int32, (1, 128), 1) % HALF
         query_start = jnp.zeros((1, 128), jnp.int32)
         for end in ends:
             query_start = jnp.where(end <= query_pos, end, query_start)
-
-        def score(t, count, rows, top):
-            s = lax.dot_general(window(0, half, t, count), q8[half], NT, preferred_element_type=F32)
-            key_pos = (blocks[half] - (WINDOW - 1) + t) * HALF + lax.broadcasted_iota(jnp.int32, (count * HALF, 128), 0)
-            bias = jnp.where((key_pos >= query_start) & (key_pos <= query_pos), 0.0, HIDDEN)
-            s = s * (SCALE * LOG2E) + jnp.concatenate([bias] * (QCOLS // 128), axis=1)
-            p_buf[half, rows] = s
-            return jnp.maximum(top, jnp.max(fold(s), axis=0))
-
-        top = each_step(score, jnp.full((8, QCOLS), HIDDEN, F32))
-        top = jnp.max(top, axis=0, keepdims=True)
-
-        def weigh(t, count, rows, total):
-            p = jnp.exp2(p_buf[half, rows] - top)
-            p_buf[half, rows] = p
-            return total + jnp.sum(fold(p), axis=0)
-
-        total = each_step(weigh, jnp.zeros((8, QCOLS), F32))
-        inverse = 1.0 / jnp.sum(total, axis=0, keepdims=True)
-
-        def value_terms(t, count, rows, carry):
-            pb = (p_buf[half, rows] * inverse).astype(BF16)
-            dv = jnp.dot(pb, d8[half], preferred_element_type=F32)
-            acc[1, half, pl.ds(1 + t, count)] = dv.reshape(count, HALF, HD)
-            return carry
-
-        each_step(value_terms, 0)
-        return inverse
-
-    def key_terms(half, inverse):
-        def prob_grads(t, count, rows, dot):
-            g = lax.dot_general(window(1, half, t, count), d8[half], NT, preferred_element_type=F32)
-            g_buf[rows] = g
-            return dot + jnp.sum(fold(p_buf[half, rows] * g), axis=0)
-
-        dot = each_step(prob_grads, jnp.zeros((8, QCOLS), F32))
-        delta = jnp.sum(dot, axis=0, keepdims=True) * inverse
-
-        def terms(t, count, rows, carry):
-            ds = (p_buf[half, rows] * inverse * (g_buf[rows] - delta)).astype(BF16)
-            ds_buf[half, rows] = ds
-            dk = jnp.dot(ds, q8[half], preferred_element_type=F32) * SCALE
-            acc[0, half, pl.ds(1 + t, count)] = dk.reshape(count, HALF, HD)
-            return carry
-
-        each_step(terms, 0)
+        return query_start, query_pos
+
+    def scores():
+        spans = [query_span(half) for half in range(2)]
+        top = [jnp.full((8, QCOLS), HIDDEN, F32)] * 2
+        for t, count, rows in STEPS:
+            for half in range(2):
+                s = lax.dot_general(window(0, half, t, count), q8[half], NT, preferred_element_type=F32)
+                key_pos = (blocks[half] - (WINDOW - 1) + t) * HALF + lax.broadcasted_iota(jnp.int32, (count * HALF, 128), 0)
+                bias = jnp.where((key_pos >= spans[half][0]) & (key_pos <= spans[half][1]), 0.0, HIDDEN)
+                s = s * (SCALE * LOG2E) + jnp.concatenate([bias] * (QCOLS // 128), axis=1)
+                p_buf[half, rows] = s
+                top[half] = jnp.maximum(top[half], jnp.max(fold(s), axis=0))
+        return [jnp.max(top[half], axis=0, keepdims=True) for half in range(2)]
+
+    def weigh(top):
+        total = [jnp.zeros((8, QCOLS), F32)] * 2
+        for t, count, rows in STEPS:
+            for half in range(2):
+                p = jnp.exp2(p_buf[half, rows] - top[half])
+                p_buf[half, rows] = p
+                total[half] = total[half] + jnp.sum(fold(p), axis=0)
+        return [1.0 / jnp.sum(total[half], axis=0, keepdims=True) for half in range(2)]
+
+    def value_terms(inverse):
+        for t, count, rows in STEPS:
+            for half in range(2):
+                pb = (p_buf[half, rows] * inverse[half]).astype(BF16)
+                dv = jnp.dot(pb, d8[half], preferred_element_type=F32)
+                acc[1, half, 1 + t : 1 + t + count] = dv.reshape(count, HALF, HD)
+
+    def key_terms(inverse):
+        dot = [jnp.zeros((8, QCOLS), F32)] * 2
+        for t, count, rows in STEPS:
+            for half in range(2):
+                g = lax.dot_general(window(1, half, t, count), d8[half], NT, preferred_element_type=F32)
+                g_buf[half, rows] = g
+                dot[half] = dot[half] + jnp.sum(fold(p_buf[half, rows] * g), axis=0)
+        delta = [jnp.sum(dot[half], axis=0, keepdims=True) * inverse[half] for half in range(2)]
+        for t, count, rows in STEPS:
+            for half in range(2):
+                ds = (p_buf[half, rows] * inverse[half] * (g_buf[half, rows] - delta[half])).astype(BF16)
+                ds_buf[half, rows] = ds
+                dk = jnp.dot(ds, q8[half], preferred_element_type=F32) * SCALE
+                acc[0, half, 1 + t : 1 + t + count] = dk.reshape(count, HALF, HD)
 
     def query_terms(half):
-        def terms(t, count, rows, total):
-            return total + lax.dot_general(window(0, half, t, count), ds_buf[half, rows], TN, preferred_element_type=F32)
-
-        dq = (each_step(terms, jnp.zeros((HD, QCOLS), F32)) * SCALE).T
+        total = jnp.zeros((HD, QCOLS), F32)
+        for t, count, rows in STEPS:
+            total = total + lax.dot_general(window(0, half, t, count), ds_buf[half, rows], TN, preferred_element_type=F32)
+        dq = (total * SCALE).T
         for h in range(HEADS):
             dq_ref[0, half * HALF : (half + 1) * HALF, h * HD : (h + 1) * HD] = dq[h * HALF : (h + 1) * HALF].astype(BF16)
 
-    def in_stored_order(w, core, t):
-        def body(i, carry):
-            for part_half in range(2):
-                block = order_ref[2 * ((t * NZL + i) * NC + core) + part_half]
-                both = [acc[w, h, jnp.clip(block - blocks[h] + WINDOW, 0, WINDOW + 1)] for h in range(2)]
-                part[w, core, t, i, part_half * HALF : (part_half + 1) * HALF] = (both[0] + both[1]).astype(BF16)
-            return carry
-
-        lax.fori_loop(0, NZL, body, 0)
+    def stored_half(w, r, part_half):
+        block = order_ref[2 * r + part_half]
+        both = [acc[w, h, jnp.clip(block - blocks[h] + WINDOW, 0, WINDOW + 1)] for h in range(2)]
+        return both[0] + both[1]
 
     def sum_to_core(w):
-        for o in (2, 1, 3, 0):
-            t = (y + o) % NY
-            in_stored_order(w, 1 - c, t)
-            go(part.at[w, 1 - c, t], theirs.at[w, t], c_s.at[w, o], c_r.at[w, o], sibling)
-        for o in (2, 1, 3, 0):
-            in_stored_order(w, c, (y + o) % NY)
+        for oz in (2, 1, 3, 0):
+            tz = (zl + oz) % NZL
+
+            def body(i, carry):
+                for part_half in range(2):
+                    rows = slice(part_half * HALF, (part_half + 1) * HALF)
+                    part[w, tz, i, rows] = stored_half(w, (i * NZL + tz) * NC + 1 - c, part_half).astype(BF16)
+                return carry
+
+            lax.fori_loop(0, NY, body, 0)
+            go(part.at[w, tz], theirs.at[w, tz], c_s.at[w, oz], c_r.at[w, oz], sibling)
 
     def sum_to_y(w):
-        for o in (2, 1, 3, 0):
-            t = (y + o) % NY
-            arrived(theirs.at[w, t], c_s.at[w, o], c_r.at[w, o], sibling)
-            for oz in (2, 1, 3, 0):
-                tz = (zl + oz) % NZL
-                part[w, c, t, tz] = (part[w, c, t, tz].astype(F32) + theirs[w, t, tz].astype(F32)).astype(BF16)
+        for oz in (2, 1, 3, 0):
+            tz = (zl + oz) % NZL
+            arrived(theirs.at[w, tz], c_s.at[w, oz], c_r.at[w, oz], sibling)
+            for o in (2, 1, 3, 0):
+                t = (y + o) % NY
+                for part_half in range(2):
+                    rows = slice(part_half * HALF, (part_half + 1) * HALF)
+                    total = stored_half(w, (t * NZL + tz) * NC + c, part_half) + theirs[w, tz, t, rows].astype(F32)
+                    if o:
+                        y_out[w, o - 1, oz, rows] = total.astype(BF16)
+                    else:
+                        y_own[w, oz, rows] = total
                 if o:
-                    go(part.at[w, c, t, tz], y_in.at[w, o - 1, oz], y_s.at[w, o - 1, oz], y_r.at[w, o - 1, oz], y_peers[o - 1])
+                    go(y_out.at[w, o - 1, oz], y_in.at[w, o - 1, oz], y_s.at[w, o - 1, oz], y_r.at[w, o - 1, oz], y_peers[o - 1])
 
     def sum_to_z(w):
         for oz in (2, 1, 3, 0):
-            total = part[w, c, y, (zl + oz) % NZL].astype(F32)
+            total = y_own[w, oz]
             for o in (1, 3, 2):
                 arrived(y_in.at[w, o - 1, oz], y_s.at[w, o - 1, oz], y_r.at[w, o - 1, oz], y_peers[o - 1])
                 total = total + y_in[w, o - 1, oz].astype(F32)
@@ -323,14 +334,20 @@
             total = total + z_in[w, oz - 1].astype(F32)
         rounded = total.astype(BF16)
         g_all[w, slot] = rounded
-        for o in XS:
-            go(g_all.at[w, slot], g_all.at[w, slot], g_s.at[w, o - 1], g_r.at[w, o - 1], xc_peers[o - 1])
+        for o in (2, 1, 3):
+            go(g_all.at[w, slot], g_all.at[w, slot], g_s.at[w, o - 1], g_r.at[w, o - 1], x_peers[o - 1])
+        go(g_all.at[w, slot], g_all.at[w, slot], gs_s.at[w, 0], gs_r.at[w, 0], sibling)
         out_ref[0] = rounded
 
+    def x_to_core(w):
+        for o in (1, 3, 2):
+            t = ((x - o + NX) % NX) * NC + c
+            arrived(g_all.at[w, t], g_s.at[w, o - 1], g_r.at[w, o - 1], x_peers[o - 1])
+            go(g_all.at[w, t], g_all.at[w, t], gs_s.at[w, o], gs_r.at[w, o], sibling)
+
     def product(w):
-        for o in XR:
-            t = xc_from[o - 1]
-            arrived(g_all.at[w, t], g_s.at[w, o - 1], g_r.at[w, o - 1], xc_peers[o - 1])
+        for o in range(NX):
+            arrived(g_all.at[w, ((x - o + NX) % NX) * NC + 1 - c], gs_s.at[w, o], gs_r.at[w, o], sibling)
         right = jnp.concatenate([g_all[w, t] for t in range(XC)], axis=0)
         for o in (2, 1, 3, 0):
             rows = pl.ds(pl.multiple_of(((y + o) % NY) * 256, 256), 256)
@@ -358,22 +375,24 @@
             total = total + w_in[w, o - 1].astype(F32)
         wg_ref[0, :, w * HD : (w + 1) * HD] = total * (1.0 / math.sqrt(8 * SEQ))
 
-    inverses = [softmax(half) for half in range(2)]
+    top = scores()
+    for p in (1, 3, 2):
+        relay(1, p)
+    inverse = weigh(top)
+    value_terms(inverse)
     sum_to_core(1)
     for p in (0, 1, 3, 2):
-        for q in (1, 3, 2):
-            from_y(1, q, p)
-            to_core(1, q, p)
+        relayed(1, p)
     sum_to_y(1)
     from_core(1)
-    for half in range(2):
-        key_terms(half, inverses[half])
+    key_terms(inverse)
     sum_to_core(0)
+    sum_to_y(0)
     v_total = sum_to_z(1)
-    sum_to_y(0)
+    query_terms(0)
     sum_to_x(1, v_total, vg_ref)
-    for half in range(2):
-        query_terms(half)
+    query_terms(1)
+    x_to_core(1)
     k_total = sum_to_z(0)
     keep_x.wait()
     for o in XR:
@@ -382,6 +401,7 @@
     product(1)
     sum_to_x(0, k_total, kg_ref)
     product_to_z(1)
+    x_to_core(0)
     product(0)
     finish(1)
     product_to_z(0)
@@ -390,6 +410,15 @@
         copy.wait_send()
 
 
+def write_kernel(*refs):
+    sems = refs[-1]
+    copies = [pltpu.make_async_copy(refs[i], refs[i + 4], sems.at[i]) for i in range(4)]
+    for copy in copies:
+        copy.start()
+    for copy in copies:
+        copy.wait()
+
+
 def per_device(layer_input, queries, keys, values, d_out, doc_lengths, block_order):
     vmem = pl.BlockSpec(memory_space=pltpu.VMEM)
     smem = pl.BlockSpec(memory_space=pltpu.SMEM)
@@ -402,14 +431,15 @@
         return pltpu.VMEM(shape, dtype)
 
     operands = (doc_lengths, block_order, block_order.reshape(1, BLOCKS), keys, values, layer_input, queries, d_out)
-    dq, kg, vg, wg = pl.pallas_call(
+    results = (
+        jax.ShapeDtypeStruct((1, ROWS, HEADS * HD), BF16),
+        jax.ShapeDtypeStruct((1, ROWS, HD), BF16),
+        jax.ShapeDtypeStruct((1, ROWS, HD), BF16),
+        jax.ShapeDtypeStruct((1, 32, 2 * HD), F32),
+    )
+    made = pl.pallas_call(
         kernel,
-        out_shape=(
-            jax.ShapeDtypeStruct((1, ROWS, HEADS * HD), BF16),
-            jax.ShapeDtypeStruct((1, ROWS, HD), BF16),
-            jax.ShapeDtypeStruct((1, ROWS, HD), BF16),
-            jax.ShapeDtypeStruct((1, 32, 2 * HD), F32),
-        ),
+        out_shape=results,
         in_specs=[smem, smem, vmem, hbm, hbm, hbm, hbm, hbm],
         out_specs=(vmem, vmem, vmem, vmem),
         scratch_shapes=[
@@ -425,11 +455,13 @@
             buf(2, QCOLS, HD),
             buf(2, QCOLS, HD),
             buf(2, WINDOW * HALF, QCOLS, dtype=F32),
-            buf(WINDOW * HALF, QCOLS, dtype=F32),
+            buf(2, WINDOW * HALF, QCOLS, dtype=F32),
             buf(2, WINDOW * HALF, QCOLS),
             buf(2, 2, WINDOW + 2, HALF, HD, dtype=F32),
-            buf(2, NC, NY, NZL, ROWS, HD),
-            buf(2, NY, NZL, ROWS, HD),
+            buf(2, NZL, NY, ROWS, HD),
+            buf(2, NZL, NY, ROWS, HD),
+            buf(2, NY - 1, NZL, ROWS, HD),
+            buf(2, NZL, ROWS, HD, dtype=F32),
             buf(2, NY - 1, NZL, ROWS, HD),
             buf(2, NZL - 1, ROWS, HD),
             buf(2, NZL - 1, ROWS, HD),
@@ -440,13 +472,21 @@
             buf(2, NZL * NZH, 32, HD),
             buf(2, NZL * NZH - 1, 32, HD),
             pltpu.SemaphoreType.DMA((8,)),
-            *dma(2, 3), *dma(2, 4, 3), *dma(2, 4, 4), *dma(7), *dma(2, 4), *dma(2, 3, 4), *dma(2, 3),
-            *dma(2, 7), *dma(2, 3), *dma(2, 7),
+            *dma(2, 3), *dma(2, 4, 3), *dma(2, 4, 2), *dma(2, 4, 4), *dma(7), *dma(2, 4), *dma(2, 3, 4), *dma(2, 3),
+            *dma(2, 3), *dma(2, 4), *dma(2, 3), *dma(2, 7),
         ],
         compiler_params=pltpu.CompilerParams(collective_id=0, has_side_effects=True, vmem_limit_bytes=48 << 20),
         name="backward",
     )(*(pltpu.with_memory_space_constraint(a, pltpu.HBM) for a in operands))
-    return dq, kg, vg, wg
+    return pl.pallas_call(
+        write_kernel,
+        out_shape=results,
+        in_specs=[vmem] * 4,
+        out_specs=(hbm,) * 4,
+        scratch_shapes=[pltpu.SemaphoreType.DMA((4,))],
+        compiler_params=pltpu.CompilerParams(vmem_limit_bytes=4 << 20),
+        name="write",
+    )(*made)
 
 
 def solution(mesh):

time: 70 us -> 66.8 us (0.954)
  local copies, waits for them, and re-layouts: 2.55 us -> 0 us
    unnamed x4 -> x0, local copies, waits for them, and re-layouts: 2.55 us -> none
    pallas_call x1 -> x2, Pallas kernels: 66.7 us -> 66.1 us  [the longest x1 65.3 us: per_device(): pl.pallas_call(kernel, out_shape=results, in_specs=[smem, smem, vmem, hbm...]
where the time goes in v3:
time: 66.8 us; the launch traced here: 66.7 us
  Pallas kernels  66.1 us (99%)
    pallas_call x1, Pallas kernels, per_device(): pl.pallas_call(kernel, out_shape=results, in_specs=[smem, smem, vmem, hbm...  65.3 us

profile of v3, /device:TPU:1, one launch (start us, length us, event | category | flops | bytes accessed | tf_op | source)
XLA Modules:
  0.0 66.7 jit_solution(8960254855874697340)
XLA Ops:
  0.6 65.3 %backward.1 = (bf16[1,128,1024]{2,1,0:T(8,128)(2,1)S(1)}, bf16[1,128,128]{2,1,0:T(8,128)(2,1)S(1)}, bf16[1,128,128]{2,1,0:T(8,128)(2,1)S(1)}, f32[1,32,256]{2,1,0:T(8,128)S(1)}) custom-call(s32[1,8]{1,0:T(1,128)} %doc_ref.1, s32[64]{0:T(128)} %order_ref.1, s32[1,64]{1,0:T(1,128)} %bitcast.1, bf16[1,128,128]{2,1,0:T(8,128)(2,1)} %k_hbm.1, ...), custom_call_target="tpu_custom_call" | custom-call | tf_op jit(solution)/shard_map/backward/pallas_call | solution.py:440
  66.0 0.8 %write.1 = (bf16[1,128,1024]{2,1,0:T(8,128)(2,1)}, bf16[1,128,128]{2,1,0:T(8,128)(2,1)}, bf16[1,128,128]{2,1,0:T(8,128)(2,1)}, f32[1,32,256]{2,1,0:T(8,128)}) custom-call(bf16[1,128,1024]{2,1,0:T(8,128)(2,1)S(1)} %get-tuple-element.8.refs_0_, bf16[1,128,128]{2,1,0:T(8,128)(2,1)S(1)} %get-tuple-element.9.refs_1_, ...), custom_call_target="tpu_custom_call" | custom-call | tf_op jit(solution)/shard_map/write/pallas_call | solution.py:481

commit v4 on v3

--- a/solution.py
+++ b/solution.py
@@ -48,18 +48,11 @@
     )
 
 
-def greet(peers):
-    barrier = pltpu.get_barrier_semaphore()
-    for peer in peers:
-        pl.semaphore_signal(barrier, inc=1, device_id=peer, device_id_type=MESH)
-    pl.semaphore_wait(barrier, len(peers))
-
-
 def kernel(
     doc_ref, order_ref, order_row, k_hbm, v_hbm, x_hbm, q_hbm, d_hbm, dq_ref, kg_ref, vg_ref, wg_ref,
     stored, stored_v, k_all, v_all, xv, xt, x_in, q_in, d_in, q8, d8, p_buf, g_buf, ds_buf, acc, part,
     theirs, y_out, y_own, y_in, z_out, z_in, g_all, p_out, p_in, w_acc, w_out, w_in, local,
-    gz_s, gz_r, gy_s, gy_r, gh_s, gh_r, gc_s, gc_r, a_s, a_r, c_s, c_r, y_s, y_r, z_s, z_r, g_s, g_r, gs_s, gs_r, p_s, p_r, w_s, w_r,
+    gz_s, gz_r, gy_s, gy_r, gc_s, gc_r, a_s, a_r, c_s, c_r, y_s, y_r, z_s, z_r, g_s, g_r, gs_s, gs_r, p_s, p_r, w_s, w_r,
 ):
     x, zh, y, zl, c = place()
     kv = (k_all, v_all)
@@ -91,7 +84,29 @@
     x_peers = [device((x + o) % NX, zh, y, zl, c) for o in range(1, NX)]
     zz_to = [(zz + o) % (NZH * NZL) for o in range(1, NZH * NZL)]
     zz_peers = [device(x, t // NZL, y, t % NZL, c) for t in zz_to]
-    greet(xc_peers + y_peers + zz_peers)
+    barrier = pltpu.get_barrier_semaphore()
+    peers = xc_peers + y_peers + zz_peers
+    for peer in peers:
+        pl.semaphore_signal(barrier, inc=1, device_id=peer, device_id_type=MESH)
+
+    to_row = lax.broadcasted_iota(jnp.int32, (256, 256), 0)
+    from_row = lax.broadcasted_iota(jnp.int32, (256, 256), 1)
+    group = to_row // 64
+    source = (group % 2) * 128 + (group // 2) * 64 + to_row % 64
+    pick = jnp.where(source == from_row, 1.0, 0.0).astype(BF16)
+
+    def turn(core, xh):
+        for k in range(NY * NZL // 2):
+            at = 2 * k * 512 + core * 256 + xh * 128
+            pair = jnp.concatenate([xv[:, at : at + 128], xv[:, at + 512 : at + 640]], axis=1)
+            turned = lax.dot_general(pick, pair, NT, preferred_element_type=F32).astype(BF16)
+            xt[(2 * xh) * NC + core, k * 128 : (k + 1) * 128, :] = turned[:128]
+            xt[(2 * xh + 1) * NC + core, k * 128 : (k + 1) * 128, :] = turned[128:]
+
+    loads[4].wait()
+    turn(0, 0)
+    turn(0, 1)
+    pl.semaphore_wait(barrier, len(peers))
     sends = []
 
     def go(src, dst, send, recv, to):
@@ -99,11 +114,14 @@
         copy.start()
         sends.append(copy)
 
+    def spread(t):
+        at = (t - slot + XC) % XC - 1
+        go(xt.at[t], x_in.at[slot], a_s.at[at], a_r.at[at], device(t // NC, zh, y, zl, t % NC))
+
     def arrived(dst, send, recv, to):
         remote(dst, dst, send, recv, to).wait_recv()
 
     Z = (2, 1, 3)
-    XS = (4, 2, 6, 3, 5, 1, 7)
     XR = (1, 7, 2, 3, 5, 6, 4)
 
     def to_z(w):
@@ -112,21 +130,14 @@
 
     def to_y(w, p):
         r = rank(0, p, c)
-        for o in (1, 3):
+        for o in (2, 1, 3):
             go(kv[w].at[r], kv[w].at[r], gy_s.at[w, p, o - 1], gy_r.at[w, p, o - 1], y_peers[o - 1])
 
-    def relay(w, p):
-        for q, half in ((1, 0), (3, 1)):
+    def from_y(w, p):
+        for q in (1, 3, 2):
             r = rank(q, p, c)
             arrived(kv[w].at[r], gy_s.at[w, p, q - 1], gy_r.at[w, p, q - 1], y_peers[q - 1])
-            go(kv[w].at[r, half], kv[w].at[r, half], gh_s.at[w, p, half], gh_r.at[w, p, half], y_peers[q - 1])
             to_core(w, q, p)
-
-    def relayed(w, p):
-        r = rank(2, p, c)
-        for q, half in ((1, 0), (3, 1)):
-            arrived(kv[w].at[r, half], gh_s.at[w, p, half], gh_r.at[w, p, half], y_peers[q - 1])
-        to_core(w, 2, p)
 
     def to_core(w, q, p):
         r = rank(q, p, c)
@@ -147,8 +158,6 @@
     to_core(0, 0, 0)
     loads[2].wait()
     loads[3].wait()
-    to_y(1, 0)
-    to_core(1, 0, 0)
 
     same = order_row[...] == lax.broadcasted_iota(jnp.int32, (BLOCKS, BLOCKS), 0)
     column = lax.broadcasted_iota(jnp.int32, (BLOCKS, BLOCKS), 1)
@@ -157,42 +166,26 @@
     load_stored = pltpu.make_async_copy(stored_v, stored, local.at[7])
     load_stored.start()
 
-    to_row = lax.broadcasted_iota(jnp.int32, (256, 256), 0)
-    from_row = lax.broadcasted_iota(jnp.int32, (256, 256), 1)
-    group = to_row // 64
-    source = (group % 2) * 128 + (group // 2) * 64 + to_row % 64
-    pick = jnp.where(source == from_row, 1.0, 0.0).astype(BF16)
-
-    def turn(core, xh):
-        for k in range(NY * NZL // 2):
-            at = 2 * k * 512 + core * 256 + xh * 128
-            pair = jnp.concatenate([xv[:, at : at + 128], xv[:, at + 512 : at + 640]], axis=1)
-            turned = lax.dot_general(pick, pair, NT, preferred_element_type=F32).astype(BF16)
-            xt[(2 * xh) * NC + core, k * 128 : (k + 1) * 128, :] = turned[:128]
-            xt[(2 * xh + 1) * NC + core, k * 128 : (k + 1) * 128, :] = turned[128:]
-
-    loads[4].wait()
-    turn(0, 0)
-    turn(0, 1)
-    to_z(1)
+    for o in (2, 1, 3):
+        spread((x + o) % NX * NC)
     for p in (1, 3, 2):
         from_z(0, p)
         to_y(0, p)
         to_core(0, 0, p)
-    relay(0, 0)
     turn(1, 0)
     turn(1, 1)
+    for o in (2, 1, 3):
+        spread((x + o) % NX * NC + 1)
+    spread(x * NC + 1 - c)
     keep_x = pltpu.make_async_copy(xt.at[slot], x_in.at[slot], local.at[4])
     keep_x.start()
-    for o in XS:
-        go(xt.at[xc_to[o - 1]], x_in.at[slot], a_s.at[o - 1], a_r.at[o - 1], xc_peers[o - 1])
-    for p in (1, 3, 2):
-        relay(0, p)
+    to_z(1)
+    to_y(1, 0)
+    to_core(1, 0, 0)
     for p in (1, 3, 2):
         from_z(1, p)
         to_y(1, p)
         to_core(1, 0, p)
-    relay(1, 0)
     for w in range(2):
         for half in range(2):
             acc[w, half, 0] = jnp.zeros((HALF, HD), F32)
@@ -211,7 +204,7 @@
         ends.append(end)
     blocks = [order_ref[2 * me + half] for half in range(2)]
     for p in (0, 1, 3, 2):
-        relayed(0, p)
+        from_y(0, p)
     from_core(0)
 
     STEPS = [(t, min(STEP, WINDOW - t), slice(t * HALF, min(t + STEP, WINDOW) * HALF)) for t in range(0, WINDOW, STEP)]
@@ -376,13 +369,11 @@
         wg_ref[0, :, w * HD : (w + 1) * HD] = total * (1.0 / math.sqrt(8 * SEQ))
 
     top = scores()
-    for p in (1, 3, 2):
-        relay(1, p)
     inverse = weigh(top)
     value_terms(inverse)
     sum_to_core(1)
     for p in (0, 1, 3, 2):
-        relayed(1, p)
+        from_y(1, p)
     sum_to_y(1)
     from_core(1)
     key_terms(inverse)
@@ -400,11 +391,11 @@
         arrived(x_in.at[t], a_s.at[o - 1], a_r.at[o - 1], xc_peers[o - 1])
     product(1)
     sum_to_x(0, k_total, kg_ref)
-    product_to_z(1)
     x_to_core(0)
     product(0)
+    product_to_z(1)
+    product_to_z(0)
     finish(1)
-    product_to_z(0)
     finish(0)
     for copy in sends:
         copy.wait_send()
@@ -472,7 +463,7 @@
             buf(2, NZL * NZH, 32, HD),
             buf(2, NZL * NZH - 1, 32, HD),
             pltpu.SemaphoreType.DMA((8,)),
-            *dma(2, 3), *dma(2, 4, 3), *dma(2, 4, 2), *dma(2, 4, 4), *dma(7), *dma(2, 4), *dma(2, 3, 4), *dma(2, 3),
+            *dma(2, 3), *dma(2, 4, 3), *dma(2, 4, 4), *dma(7), *dma(2, 4), *dma(2, 3, 4), *dma(2, 3),
             *dma(2, 3), *dma(2, 4), *dma(2, 3), *dma(2, 7),
         ],
         compiler_params=pltpu.CompilerParams(collective_id=0, has_side_effects=True, vmem_limit_bytes=48 << 20),

time: 66.8 us -> 63.2 us (0.946)
  Pallas kernels: 66.1 us -> 62.4 us
    pallas_call x1, Pallas kernels: 65.3 us -> 61.7 us  [per_device(): pl.pallas_call(kernel, out_shape=results, in_specs=[smem, smem, vmem, hbm...]
where the time goes in v4:
time: 63.2 us; the launch traced here: 63.1 us
  Pallas kernels  62.4 us (99%)
  between operations  0.64 us (1%)
    pallas_call x1, Pallas kernels, per_device(): pl.pallas_call(kernel, out_shape=results, in_specs=[smem, smem, vmem, hbm...  61.7 us

profile of v4, /device:TPU:1, one launch (start us, length us, event | category | flops | bytes accessed | tf_op | source)
XLA Modules:
  0.0 63.1 jit_solution(12280882606883498364)
XLA Ops:
  0.6 61.7 %backward.1 = (bf16[1,128,1024]{2,1,0:T(8,128)(2,1)S(1)}, bf16[1,128,128]{2,1,0:T(8,128)(2,1)S(1)}, bf16[1,128,128]{2,1,0:T(8,128)(2,1)S(1)}, f32[1,32,256]{2,1,0:T(8,128)S(1)}) custom-call(s32[1,8]{1,0:T(1,128)} %doc_ref.1, s32[64]{0:T(128)} %order_ref.1, s32[1,64]{1,0:T(1,128)} %bitcast.1, bf16[1,128,128]{2,1,0:T(8,128)(2,1)} %k_hbm.1, ...), custom_call_target="tpu_custom_call" | custom-call | tf_op jit(solution)/shard_map/backward/pallas_call | solution.py:431
  62.3 0.8 %write.1 = (bf16[1,128,1024]{2,1,0:T(8,128)(2,1)}, bf16[1,128,128]{2,1,0:T(8,128)(2,1)}, bf16[1,128,128]{2,1,0:T(8,128)(2,1)}, f32[1,32,256]{2,1,0:T(8,128)}) custom-call(bf16[1,128,1024]{2,1,0:T(8,128)(2,1)S(1)} %get-tuple-element.8.refs_0_, bf16[1,128,128]{2,1,0:T(8,128)(2,1)S(1)} %get-tuple-element.9.refs_1_, ...), custom_call_target="tpu_custom_call" | custom-call | tf_op jit(solution)/shard_map/write/pallas_call | solution.py:472

commit v5 on v4

--- a/solution.py
+++ b/solution.py
@@ -383,8 +383,8 @@
     query_terms(0)
     sum_to_x(1, v_total, vg_ref)
     query_terms(1)
+    k_total = sum_to_z(0)
     x_to_core(1)
-    k_total = sum_to_z(0)
     keep_x.wait()
     for o in XR:
         t = xc_from[o - 1]

time: 63.2 us -> 61.5 us (0.973)
  Pallas kernels: 62.4 us -> 60.6 us
    pallas_call x1, Pallas kernels: 61.7 us -> 59.9 us  [per_device(): pl.pallas_call(kernel, out_shape=results, in_specs=[smem, smem, vmem, hbm...]
where the time goes in v5:
time: 61.5 us; the launch traced here: 61.3 us
  Pallas kernels  60.6 us (99%)
  between operations  0.64 us (1%)
    pallas_call x1, Pallas kernels, per_device(): pl.pallas_call(kernel, out_shape=results, in_specs=[smem, smem, vmem, hbm...  59.9 us

profile of v5, /device:TPU:1, one launch (start us, length us, event | category | flops | bytes accessed | tf_op | source)
XLA Modules:
  0.0 61.3 jit_solution(6147065306213735890)
XLA Ops:
  0.6 59.9 %backward.1 = (bf16[1,128,1024]{2,1,0:T(8,128)(2,1)S(1)}, bf16[1,128,128]{2,1,0:T(8,128)(2,1)S(1)}, bf16[1,128,128]{2,1,0:T(8,128)(2,1)S(1)}, f32[1,32,256]{2,1,0:T(8,128)S(1)}) custom-call(s32[1,8]{1,0:T(1,128)} %doc_ref.1, s32[64]{0:T(128)} %order_ref.1, s32[1,64]{1,0:T(1,128)} %bitcast.1, bf16[1,128,128]{2,1,0:T(8,128)(2,1)} %k_hbm.1, ...), custom_call_target="tpu_custom_call" | custom-call | tf_op jit(solution)/shard_map/backward/pallas_call | solution.py:431
  60.5 0.8 %write.1 = (bf16[1,128,1024]{2,1,0:T(8,128)(2,1)}, bf16[1,128,128]{2,1,0:T(8,128)(2,1)}, bf16[1,128,128]{2,1,0:T(8,128)(2,1)}, f32[1,32,256]{2,1,0:T(8,128)}) custom-call(bf16[1,128,1024]{2,1,0:T(8,128)(2,1)S(1)} %get-tuple-element.8.refs_0_, bf16[1,128,128]{2,1,0:T(8,128)(2,1)S(1)} %get-tuple-element.9.refs_1_, ...), custom_call_target="tpu_custom_call" | custom-call | tf_op jit(solution)/shard_map/write/pallas_call | solution.py:472
